TPU v7x, 512 devices: a whole 4x4x16 slice. The times are simulated.
512 devices in a mesh: sub: 64 (over z, x), grp: 8 (over y, core).
Axes of the slice: x: 4, y: 4, z: 16, core: 2. Of those that a mesh axis runs over, the one named last changes fastest.
Arguments:
- schur: float32 [64, 8, 1024, 1024], P('sub', 'grp'), may hold values from -0.5 to 13, as said below
- loads: float32 [64, 8, 64, 1024], P('sub', 'grp'), may hold values from -30 to 30
- block_map: int32 [64, 8, 8], P('sub', 'grp'), may hold values from 0 to 7, each once within a row
- primal_map: int32 [64, 8, 8], P('sub', 'grp'), may hold values from 0 to 31
- disk_mask: int32 [64, 8, 1024], P('sub', 'grp'), may hold values 0 or 1
Outputs:
- solution: float32 [64, 8, 64, 1024], P('sub', 'grp')
- residual: float32 [64, 8, 64, 1024], P('sub', 'grp')
Inputs may be any that keep to these rules, and one draw needn't show every extreme that they name: `schur`: each subdomain's Schur complement is symmetric with a strictly dominant positive diagonal.
All inputs are finite; a program needn't handle non-finite values. No bound on the sum of `disk_mask` on one device may be relied on, other than what follows from the above.
Results may differ from a plain program's by a relative error of at most 0.0003.
Values sent between devices are 32-bit elements; how exact they have to be, the bound alone decides.
A program may use at most 128 MiB of HBM per device.

v0:
```python
import math

import jax
import jax.numpy as jnp
from jax import lax
from jax.sharding import PartitionSpec as P

ITERS = 2


highest = lax.Precision.HIGHEST
disk_penalty = 0.1


def extended(block, sides, width):
    for axis, dim in sides:
        count = lax.axis_size(axis)
        forward = [(i, i + 1) for i in range(count - 1)]
        forward.append((count - 1, 0))
        backward = [(target, source) for source, target in forward]
        low = lax.ppermute(
            lax.slice_in_dim(block, block.shape[dim] - width, None, axis=dim), axis, forward
        )
        high = lax.ppermute(lax.slice_in_dim(block, 0, width, axis=dim), axis, backward)
        block = jnp.concatenate([low, block, high], axis=dim)
    return block


def one_hot(indices, count):
    return (indices[..., None] == jnp.arange(count, dtype=jnp.int32)).astype(jnp.float32)


def chol_apply(factor, values):
    partial_sol = lax.linalg.triangular_solve(
        factor, values, left_side=False, lower=True, transpose_a=True
    )
    return lax.linalg.triangular_solve(factor, partial_sol, left_side=False, lower=True)


def inner_local(first_vec, second_vec):
    return jnp.sum(first_vec[1] * second_vec[1], axis=1)


def residual_sum(first_vec, second_vec):
    return lax.psum(inner_local(first_vec, second_vec), ("sub", "grp"))


def direction_sum(first_vec, second_vec):
    return lax.psum(inner_local(first_vec, second_vec), ("sub", "grp"))


def body(schur, loads, block_map, primal_map, disk_mask):
    matrix = schur[0, 0]
    full_size = matrix.shape[0]
    half_size = full_size // 2
    block_width = full_size // 8
    row_count = loads.shape[2]
    coarse = 4 * lax.axis_size("grp")
    root = math.sqrt(block_width)
    penalty = disk_penalty * disk_mask[0, 0].astype(jnp.float32)
    shifted = matrix + jnp.diag(penalty)
    placing = one_hot(block_map[0, 0], 8).reshape(8, 2, 4)
    primal = one_hot(primal_map[0, 0], coarse)

    def to_local(face_vals):
        blocks = face_vals.reshape(2, row_count, 4, block_width)
        return jnp.einsum("hrqb,jhq->rjb", blocks, placing, precision=highest).reshape(
            row_count, full_size
        )

    def to_faces(local_vals):
        blocks = local_vals.reshape(row_count, 8, block_width)
        return jnp.einsum("rjb,jhq->hrqb", blocks, placing, precision=highest).reshape(
            2, row_count, half_size
        )

    def assemble(face_vals):
        padded = extended(face_vals, (("sub", 0),), 1)
        return jnp.stack([padded[0] + padded[1], padded[2] + padded[3]])

    right_side = assemble(to_faces(loads[0, 0]))
    factor = jnp.linalg.cholesky(shifted)
    block_sums = shifted.reshape(8, block_width, 8, block_width).sum(axis=(1, 3)) / block_width
    local_coarse = jnp.dot(
        primal.T, jnp.dot(block_sums, primal, precision=highest), precision=highest
    )
    coarse_matrix = jnp.eye(coarse, dtype=jnp.float32) + lax.psum(local_coarse, "grp")
    coarse_factor = jnp.linalg.cholesky(coarse_matrix)

    def precondition(face_vals):
        weighted = 0.5 * to_local(face_vals)
        solved = chol_apply(factor, weighted)
        averages = weighted.reshape(row_count, 8, block_width).sum(axis=2) / root
        coarse_rhs = lax.psum(jnp.dot(averages, primal, precision=highest), "grp")
        amounts = chol_apply(coarse_factor, coarse_rhs)
        spread = jnp.dot(amounts, primal.T, precision=highest) / root
        correction = jnp.broadcast_to(spread[:, :, None], (row_count, 8, block_width)).reshape(
            row_count, full_size
        )
        return assemble(to_faces(0.5 * (solved + correction)))

    solution = jnp.zeros_like(right_side)
    residual = right_side
    precond = precondition(residual)
    direction = precond
    energy = residual_sum(residual, precond)
    for iteration in range(ITERS):
        product = jnp.dot(to_local(direction), shifted, precision=highest)
        image = assemble(to_faces(product))
        alpha = (energy / direction_sum(direction, image))[None, :, None]
        solution = solution + alpha * direction
        residual = residual - alpha * image
        if iteration + 1 < ITERS:
            precond = precondition(residual)
            fresh = residual_sum(residual, precond)
            direction = precond + (fresh / energy)[None, :, None] * direction
            energy = fresh
    solution_out = jnp.concatenate([solution[0], solution[1]], axis=1)[None, None]
    residual_out = jnp.concatenate([residual[0], residual[1]], axis=1)[None, None]
    return (solution_out, residual_out)


def solution(mesh):
    in_specs = (
        P("sub", "grp", None, None),
        P("sub", "grp", None, None),
        P("sub", "grp", None),
        P("sub", "grp", None),
        P("sub", "grp", None),
    )
    out_specs = (P("sub", "grp", None, None), P("sub", "grp", None, None))
    return jax.shard_map(body, mesh=mesh, in_specs=in_specs, out_specs=out_specs, check_vma=False)
```

profile of v0, /device:TPU:1, one launch (start us, length us, event | category | flops | bytes accessed | tf_op | source)
XLA Modules:
  0.0 813.4 jit_solution(10439211370959881771)
XLA Ops:
  2.7 14.1 %collective-permute-start = (f32[1,64,512]{2,1,0:T(8,128)S(1)}, f32[1,64,512]{2,1,0:T(8,128)S(1)}, u32[]{:S(2)}, u32[]{:S(2)}) collective-permute-start(f32[1,64,512]{2,1,0:T(8,128)S(1)} %slice.415), channel_id=1, source_target_pairs={{8,0},{16,8},{24,16},{32,24},{40,32},{48,40},{56,48},{64,56},{72,6... | collective-permute-start | bytes 393224 | tf_op jit(solution)/shard_map/ppermute | solution.py:24
  16.9 1.9 collective-permute-start.1
  19.6 5.3 copy.31
  24.9 4.8 bitcast_add_fusion.2
  29.7 5.3 copy.32
  35.1 4.4 fusion.1
  39.5 2.0 copy-done.3
  41.5 11.7 %cholesky.238 = f32[128,128]{1,0:T(8,128)S(1)} custom-call(f32[128,128]{1,0:T(8,128)S(1)} %cholesky.619), custom_call_target="Cholesky" | custom-call | tf_op jit(solution)/shard_map/jit(cholesky)/cholesky | solution.py:82
  53.2 9.8 %custom-call.74 = f32[1,128,128]{1,2,0:T(8,128)S(1)} custom-call(f32[1,128,128]{2,1,0:T(8,128)S(1)} %get-tuple-element.112), custom_call_target="InvertDiagBlocksLowerTriangular" | custom-call | tf_op jit(solution)/shard_map/jit(cholesky)/cholesky | solution.py:82
  63.0 1.5 fusion.10
  64.6 1.6 convolution_subtract_fusion
  66.5 11.7 %cholesky.261 = f32[128,128]{1,0:T(8,128)S(1)} custom-call(f32[128,128]{1,0:T(8,128)S(1)} %cholesky.623), custom_call_target="Cholesky" | custom-call | tf_op jit(solution)/shard_map/jit(cholesky)/cholesky | solution.py:82
  78.7 9.8 %custom-call.75 = f32[1,128,128]{1,2,0:T(8,128)S(1)} custom-call(f32[1,128,128]{2,1,0:T(8,128)S(1)} %get-tuple-element.110), custom_call_target="InvertDiagBlocksLowerTriangular" | custom-call | tf_op jit(solution)/shard_map/jit(cholesky)/cholesky | solution.py:82
  89.6 2.0 copy-done
  91.6 2.4 convolution_subtract_fusion.1
  94.0 11.7 %cholesky.497 = f32[128,128]{1,0:T(8,128)S(1)} custom-call(f32[128,128]{1,0:T(8,128)S(1)} %cholesky.628), custom_call_target="Cholesky" | custom-call | tf_op jit(solution)/shard_map/jit(cholesky)/cholesky | solution.py:82
  106.5 9.8 %custom-call.76 = f32[1,128,128]{1,2,0:T(8,128)S(1)} custom-call(f32[1,128,128]{2,1,0:T(8,128)S(1)} %get-tuple-element.108), custom_call_target="InvertDiagBlocksLowerTriangular" | custom-call | tf_op jit(solution)/shard_map/jit(cholesky)/cholesky | solution.py:82
  117.5 3.3 convolution_subtract_fusion.2
  120.8 11.7 %cholesky.516 = f32[128,128]{1,0:T(8,128)S(1)} custom-call(f32[128,128]{1,0:T(8,128)S(1)} %cholesky.633), custom_call_target="Cholesky" | custom-call | tf_op jit(solution)/shard_map/jit(cholesky)/cholesky | solution.py:82
  133.3 9.8 %custom-call.77 = f32[1,128,128]{1,2,0:T(8,128)S(1)} custom-call(f32[1,128,128]{2,1,0:T(8,128)S(1)} %get-tuple-element.106), custom_call_target="InvertDiagBlocksLowerTriangular" | custom-call | tf_op jit(solution)/shard_map/jit(cholesky)/cholesky | solution.py:82
  144.3 3.1 convolution_subtract_fusion.3
  147.4 11.9 %cholesky.535 = f32[128,128]{1,0:T(8,128)S(1)} custom-call(f32[128,128]{1,0:T(8,128)S(1)} %cholesky.638), custom_call_target="Cholesky" | custom-call | tf_op jit(solution)/shard_map/jit(cholesky)/cholesky | solution.py:82
  160.1 9.8 %custom-call.78 = f32[1,128,128]{1,2,0:T(8,128)S(1)} custom-call(f32[1,128,128]{2,1,0:T(8,128)S(1)} %get-tuple-element.104), custom_call_target="InvertDiagBlocksLowerTriangular" | custom-call | tf_op jit(solution)/shard_map/jit(cholesky)/cholesky | solution.py:82
  171.1 3.2 convolution_subtract_fusion.4
  174.3 11.7 %cholesky.555 = f32[128,128]{1,0:T(8,128)S(1)} custom-call(f32[128,128]{1,0:T(8,128)S(1)} %cholesky.643), custom_call_target="Cholesky" | custom-call | tf_op jit(solution)/shard_map/jit(cholesky)/cholesky | solution.py:82
  186.8 9.8 %custom-call.79 = f32[1,128,128]{1,2,0:T(8,128)S(1)} custom-call(f32[1,128,128]{2,1,0:T(8,128)S(1)} %get-tuple-element.102), custom_call_target="InvertDiagBlocksLowerTriangular" | custom-call | tf_op jit(solution)/shard_map/jit(cholesky)/cholesky | solution.py:82
  197.6 3.1 convolution_subtract_fusion.5
  200.8 11.7 %cholesky.575 = f32[128,128]{1,0:T(8,128)S(1)} custom-call(f32[128,128]{1,0:T(8,128)S(1)} %cholesky.648), custom_call_target="Cholesky" | custom-call | tf_op jit(solution)/shard_map/jit(cholesky)/cholesky | solution.py:82
  213.2 9.8 %custom-call.80 = f32[1,128,128]{1,2,0:T(8,128)S(1)} custom-call(f32[1,128,128]{2,1,0:T(8,128)S(1)} %get-tuple-element.100), custom_call_target="InvertDiagBlocksLowerTriangular" | custom-call | tf_op jit(solution)/shard_map/jit(cholesky)/cholesky | solution.py:82
  224.0 2.2 convolution_subtract_fusion.6
  226.2 11.7 %cholesky.593 = f32[128,128]{1,0:T(8,128)S(1)} custom-call(f32[128,128]{1,0:T(8,128)S(1)} %convolution_subtract_fusion.6), custom_call_target="Cholesky" | custom-call | tf_op jit(solution)/shard_map/jit(cholesky)/cholesky | solution.py:82
  248.3 4.9 select_select_fusion
  253.2 23.5 %while.8 = (s32[]{:T(128)}, f32[1024,1024]{0,1:T(8,128)}, s32[8,2]{0,1:T(2,128)S(1)}, f32[8,128,128]{2,1,0:T(8,128)S(1)}, s32[]{:T(128)}) while((s32[]{:T(128)}, f32[1024,1024]{0,1:T(8,128)}, s32[8,2]{0,1:T(2,128)S(1)}, f32[8,128,128]{2,1,0:T(8,128)S(1)}, s32[]{:T(128)}) %tuple.107), condition=%wide.while_cond, body=%wide.while_body.sunk | while | flops 2 | bytes 393321 | solution.py:34
  253.8 2.2 dynamic-slice.14
  256.7 2.2 dynamic-slice.14
  259.7 2.2 dynamic-slice.14
  262.6 2.2 dynamic-slice.14
  265.6 2.2 dynamic-slice.14
  268.5 2.2 dynamic-slice.14
  271.5 2.2 dynamic-slice.14
  274.4 2.1 dynamic-slice.14
  276.7 78.8 %custom-call.85 = f32[8,128,128]{1,2,0:T(8,128)S(1)} custom-call(f32[8,128,128]{2,1,0:T(8,128)S(1)} %get-tuple-element.34), custom_call_target="InvertDiagBlocksLowerTriangular" | custom-call | tf_op jit(solution)/shard_map/triangular_solve/custom-call.16 | solution.py:34
  355.5 3.2 copy.71
  358.7 3.3 fusion
  363.5 1.4 convolution_subtract_fusion.22
  377.5 23.4 %all-reduce.2 = (f32[64,32]{1,0:T(8,128)S(1)}, f32[32,32]{1,0:T(8,128)S(1)}) all-reduce(f32[64,32]{1,0:T(8,128)S(1)} %fusion.175, f32[32,32]{1,0:T(8,128)S(1)} %fusion.187), channel_id=1, replica_groups=mesh['sub'=64,'grp'=8] {'grp'}, use_global_device_ids=true, to_apply=%region_21.24 | all-reduce | flops 3072 | bytes 24576 | tf_op jit(solution)/shard_map/psum | solution.py:94
  401.0 2.9 cholesky.607
  405.3 2.4 custom-call.88
  409.1 6.7 collective-permute-start.2
  415.8 2.1 collective-permute-start.3
  418.1 6.8 collective-permute-done.3
  425.5 5.9 fusion.219
  431.9 1.9 collective-permute-start.4
  433.9 3.7 collective-permute-done.4
  438.3 1.9 collective-permute-start.5
  440.3 106.9 %all-reduce.1 = (f32[64]{0:T(128)S(1)}, f32[64]{0:T(128)S(1)}) all-reduce(f32[64]{0:T(128)S(1)} %get-tuple-element.71, f32[64]{0:T(128)S(1)} %get-tuple-element.70), channel_id=1, replica_groups=mesh['sub'=64,'grp'=8] {'sub','grp'}, use_global_device_ids=true, to_apply=%region_23.28 | all-reduce | flops 128 | bytes 1024 | tf_op jit(solution)/shard_map/psum | solution.py:45
  548.0 21.2 %psum.53 = f32[64,32]{1,0:T(8,128)S(1)} all-reduce(f32[64,32]{1,0:T(8,128)S(1)} %fusion.173), channel_id=1, replica_groups=mesh['sub'=64,'grp'=8] {'grp'}, use_global_device_ids=true, to_apply=%region_27.32 | all-reduce | flops 2048 | bytes 16384 | tf_op jit(solution)/shard_map/psum | solution.py:94
  585.4 1.9 collective-permute-start.6
  587.4 3.4 collective-permute-start.7
  591.2 104.0 %psum.54 = f32[64]{0:T(128)S(1)} all-reduce(f32[64]{0:T(128)S(1)} %fusion.59), channel_id=1, replica_groups=mesh['sub'=64,'grp'=8] {'sub','grp'}, use_global_device_ids=true, to_apply=%region_29.34 | all-reduce | flops 64 | bytes 512 | tf_op jit(solution)/shard_map/psum | solution.py:45
  695.9 5.9 fusion.220
  702.3 3.5 collective-permute-start.8
  705.8 1.9 collective-permute-start.9
  708.1 103.0 %psum.55 = f32[64]{0:T(128)S(1)} all-reduce(f32[64]{0:T(128)S(1)} %fusion.57), channel_id=1, replica_groups=mesh['sub'=64,'grp'=8] {'sub','grp'}, use_global_device_ids=true, to_apply=%region_31.36 | all-reduce | flops 64 | bytes 512 | tf_op jit(solution)/shard_map/psum | solution.py:49
  (296 shorter events, 63.2 us)
Async XLA Ops:
  2.7 359.8 %collective-permute-start = (f32[1,64,512]{2,1,0:T(8,128)S(1)}, f32[1,64,512]{2,1,0:T(8,128)S(1)}, u32[]{:S(2)}, u32[]{:S(2)}) collective-permute-start(f32[1,64,512]{2,1,0:T(8,128)S(1)} %slice.415), channel_id=1, source_target_pairs={{8,0},{16,8},{24,16},{32,24},{40,32},{48,40},{56,48},{64,56},{72,6... | collective-permute-start | bytes 393224 | tf_op jit(solution)/shard_map/ppermute | solution.py:24
  16.9 345.6 %collective-permute-start.1 = (f32[1,64,512]{2,1,0:T(8,128)S(1)}, f32[1,64,512]{2,1,0:T(8,128)S(1)}, u32[]{:S(2)}, u32[]{:S(2)}) collective-permute-start(f32[1,64,512]{2,1,0:T(8,128)S(1)} %slice.416), channel_id=1, source_target_pairs={{0,8},{8,16},{16,24},{24,32},{32,40},{40,48},{48,56},{56,64},{64,7... | collective-permute-start | bytes 393224 | tf_op jit(solution)/shard_map/ppermute | solution.py:21
  39.5 2.0 copy-start.3
  89.6 2.0 copy-start
  358.7 3.4 copy-start.5
  358.7 4.1 copy-start.4
  362.7 8.1 copy-start.1
  409.1 8.9 %collective-permute-start.2 = (f32[1,64,512]{2,1,0:T(8,128)S(1)}, f32[1,64,512]{2,1,0:T(8,128)S(1)}, u32[]{:S(2)}, u32[]{:S(2)}) collective-permute-start(f32[1,64,512]{2,1,0:T(8,128)S(1)} %slice.419), channel_id=1, source_target_pairs={{8,0},{16,8},{24,16},{32,24},{40,32},{48,40},{56,48},{64,56},{72,6... | collective-permute-start | bytes 393224 | tf_op jit(solution)/shard_map/ppermute | solution.py:24
  415.8 9.0 %collective-permute-start.3 = (f32[1,64,512]{2,1,0:T(8,128)S(1)}, f32[1,64,512]{2,1,0:T(8,128)S(1)}, u32[]{:S(2)}, u32[]{:S(2)}) collective-permute-start(f32[1,64,512]{2,1,0:T(8,128)S(1)} %slice.420), channel_id=1, source_target_pairs={{0,8},{8,16},{16,24},{24,32},{32,40},{40,48},{48,56},{56,64},{64,7... | collective-permute-start | bytes 393224 | tf_op jit(solution)/shard_map/ppermute | solution.py:21
  431.9 5.7 collective-permute-start.4
  438.3 108.9 %collective-permute-start.5 = (f32[1,64,512]{2,1,0:T(8,128)S(1)}, f32[1,64,512]{2,1,0:T(8,128)S(1)}, u32[]{:S(2)}, u32[]{:S(2)}) collective-permute-start(f32[1,64,512]{2,1,0:T(8,128)S(1)} %slice.424), channel_id=1, source_target_pairs={{0,8},{8,16},{16,24},{24,32},{32,40},{40,48},{48,56},{56,64},{64,7... | collective-permute-start | bytes 393224 | tf_op jit(solution)/shard_map/ppermute | solution.py:21
  569.9 8.8 %copy-start.2 = (f32[1024,1024]{0,1:T(8,128)S(1)}, f32[1024,1024]{0,1:T(8,128)}, u32[]{:S(2)}) copy-start(f32[1024,1024]{0,1:T(8,128)} %get-tuple-element.227) | copy-start | bytes 12582916
  585.4 5.7 collective-permute-start.6
  587.4 107.8 %collective-permute-start.7 = (f32[1,64,512]{2,1,0:T(8,128)S(1)}, f32[1,64,512]{2,1,0:T(8,128)S(1)}, u32[]{:S(2)}, u32[]{:S(2)}) collective-permute-start(f32[1,64,512]{2,1,0:T(8,128)S(1)} %slice.429), channel_id=1, source_target_pairs={{0,8},{8,16},{16,24},{24,32},{32,40},{40,48},{48,56},{56,64},{64,7... | collective-permute-start | bytes 393224 | tf_op jit(solution)/shard_map/ppermute | solution.py:21
  702.3 5.7 collective-permute-start.8
  705.8 105.4 %collective-permute-start.9 = (f32[1,64,512]{2,1,0:T(8,128)S(1)}, f32[1,64,512]{2,1,0:T(8,128)S(1)}, u32[]{:S(2)}, u32[]{:S(2)}) collective-permute-start(f32[1,64,512]{2,1,0:T(8,128)S(1)} %slice.436), channel_id=1, source_target_pairs={{0,8},{8,16},{16,24},{24,32},{32,40},{40,48},{48,56},{56,64},{64,7... | collective-permute-start | bytes 393224 | tf_op jit(solution)/shard_map/ppermute | solution.py:21
where the time goes:
time: 825 us; the launch traced here: 813 us
  blocking collectives  359 us (44%)
  other arithmetic  274 us (33%)
  matrix products  72.2 us (9%)
  local copies, waits for them, and re-layouts  49.8 us (6%)
  starting transfers between devices  39.4 us (5%)
  waiting for transfers between devices  10.9 us (1%)
    psum x2, blocking collectives, residual_sum(): return lax.psum(inner_local(first_vec, second_vec), ('sub', 'grp'))  211 us
    another operation x30, other arithmetic, body(): factor = jnp.linalg.cholesky(shifted)  167 us
    psum x1, blocking collectives, direction_sum(): return lax.psum(inner_local(first_vec, second_vec), ('sub', 'grp'))  103 us
    another operation x4, other arithmetic, chol_apply(): lax.linalg.triangular_solve(factor, values, left_side=False, lower=True,...  83.6 us
    psum x2, blocking collectives, precondition(): coarse_rhs = lax.psum(jnp.dot(averages, primal, precision=highest), 'grp')  44.7 us
    ppermute x5, starting transfers between devices, extended(): lax.ppermute(lax.slice_in_dim(block, 0, width, axis=dim), axis, backward)  28.1 us
    another operation x14, matrix products, body(): factor = jnp.linalg.cholesky(shifted)  26.4 us
    another operation x41, local copies, waits for them, and re-layouts, chol_apply(): lax.linalg.triangular_solve(factor, values, left_side=False, lower=True,...  23.2 us
  transfers between devices with their start and end apart: 10, of which 4 were waited for; matrix products, arithmetic and copies ran while one was open for 41% of the time, Pallas kernels for 0%

commit v1 on v0

v1 whole, which is shorter than its diff:
```python
import jax
import jax.numpy as jnp
from jax import lax
from jax.experimental import pallas as pl
from jax.experimental.pallas import tpu as pltpu
from jax.sharding import PartitionSpec as P

F32 = jnp.float32
BF16 = jnp.bfloat16
HI = lax.Precision.HIGHEST
MESH = pl.DeviceIdType.MESH
M = 1024
R = 64
BW = 128
NB = 8
C = 32
X_DIM = 4
ROOT = BW ** 0.5
MIB = 1 << 20


def vmem():
    return pl.BlockSpec(memory_space=pltpu.VMEM)


def smem():
    return pl.BlockSpec(memory_space=pltpu.SMEM)


def split(value):
    high = value.astype(BF16)
    low = (value - high.astype(F32)).astype(BF16)
    return high, low


def dot(a, b):
    return jnp.dot(a, b, preferred_element_type=F32)


def dot_hi(a, b, dims):
    return lax.dot_general(a, b, (dims, ((), ())), precision=HI, preferred_element_type=F32)


def spread(v):
    return jnp.broadcast_to(v, (8, BW))


def recip(a):
    r = pltpu.reciprocal(a, approx=True)
    r = r * (2.0 - a * r)
    return r * (2.0 - a * r)


def small_mm(a, b):
    out = []
    for i in range(len(a)):
        row = []
        for j in range(len(b[0])):
            t = a[i][0] * b[0][j]
            for l in range(1, len(b)):
                t = t + a[i][l] * b[l][j]
            row.append(t)
        out.append(row)
    return out


def small_inverse(d):
    n = len(d)
    if n == 2:
        a, b, e = d[0][0], d[0][1], d[1][1]
        r = recip(a * e - b * b)
        o = -(b * r)
        return [[e * r, o], [o, a * r]]
    h = n // 2
    a = small_inverse([row[:h] for row in d[:h]])
    b = [row[h:] for row in d[:h]]
    t = small_mm(a, b)
    s = [[None] * h for _ in range(h)]
    for i in range(h):
        for j in range(i, h):
            u = b[0][i] * t[0][j]
            for l in range(1, h):
                u = u + b[l][i] * t[l][j]
            s[i][j] = d[h + i][h + j] - u
            s[j][i] = s[i][j]
    s = small_inverse(s)
    ts = small_mm(t, s)
    r = [[None] * n for _ in range(n)]
    for i in range(h):
        for j in range(h):
            r[h + i][h + j] = s[i][j]
            r[i][h + j] = -ts[i][j]
            r[h + j][i] = r[i][h + j]
    for i in range(h):
        for j in range(i, h):
            u = a[i][j]
            for l in range(h):
                u = u + ts[i][l] * t[j][l]
            r[i][j] = u
            r[j][i] = u
    return r


def dense_inverse(x, n):
    groups = n // 8
    xs = [x[8 * i : 8 * i + 8, :] for i in range(groups)]
    lane = lax.broadcasted_iota(jnp.int32, (8, BW), 1)
    sub = lax.broadcasted_iota(jnp.int32, (8, BW), 0)
    for q in range(groups):
        k = 8 * q
        rows = [spread(xs[q][j : j + 1, :]) for j in range(8)]
        d = [[None] * 8 for _ in range(8)]
        for i in range(8):
            for j in range(i, 8):
                d[i][j] = spread(rows[i][:, k + j : k + j + 1])
                d[j][i] = d[i][j]
        cols = [[spread(xs[i][:, k + j : k + j + 1]) for j in range(8)] for i in range(groups)]
        r = small_inverse(d)
        p = []
        for i in range(8):
            u = r[i][0] * rows[0]
            for j in range(1, 8):
                u = u + r[i][j] * rows[j]
            for j in range(8):
                u = jnp.where(lane == k + j, r[i][j], u)
            p.append(u)
        pivots = (lane >= k) & (lane < k + 8)
        new = []
        for i in range(groups):
            if i == q:
                y = p[0]
                for j in range(1, 8):
                    y = jnp.where(sub == j, p[j], y)
            else:
                y = jnp.where(pivots, 0.0, xs[i])
                for j in range(8):
                    y = y - cols[i][j] * p[j]
            new.append(y)
        xs = new
    return jnp.concatenate(xs, 0)


def face_sources(bm_ref):
    places = [bm_ref[0, j] for j in range(NB)]
    out = []
    for f in range(NB):
        where = jnp.int32(0)
        for j in range(NB):
            where = where + jnp.where(places[j] == f, jnp.int32(j), jnp.int32(0))
        out.append(where)
    return out


def prepare_kernel(bm_ref, pm_ref, schur_ref, loads_ref, mask_ref, face_ref, tile_ref, sums):
    source = face_sources(bm_ref)
    lanes = lax.broadcasted_iota(jnp.int32, (1, M), 1) // BW
    penalty = 0.1 * mask_ref[...].astype(F32)
    sub = lax.broadcasted_iota(jnp.int32, (8, BW), 0)
    lane = lax.broadcasted_iota(jnp.int32, (8, BW), 1)
    primal = jnp.zeros((8, BW), F32)
    shifted = jnp.zeros((8, BW), F32)
    picks = []
    for f in range(NB):
        at = pl.multiple_of(source[f] * BW, BW)
        face_ref[:, f * BW : (f + 1) * BW] = loads_ref[:, pl.ds(at, BW)]
        mine = lanes == source[f]
        row = jnp.sum(schur_ref[pl.ds(at, BW), :], axis=0, keepdims=True)
        sums[f : f + 1, :] = row + jnp.where(mine, penalty, 0.0)
        picks.append(mine.astype(F32))
        coarse = pm_ref[0, source[f]]
        primal = jnp.where((sub == f) & (lane == coarse), 1.0, primal)
        shifted = jnp.where((sub == f) & (lane == coarse + C), 1.0, shifted)
    pick = jnp.concatenate(picks, 0)
    block_sums = dot_hi(sums[...], pick, ((1,), (1,))) / BW
    tile_ref[...] = dot_hi(block_sums, primal, ((1,), (0,))) + shifted


def prepare(block_map, primal_map, schur, loads, mask):
    return pl.pallas_call(
        prepare_kernel,
        out_shape=(
            jax.ShapeDtypeStruct((R, M), F32),
            jax.ShapeDtypeStruct((8, BW), F32),
        ),
        in_specs=[smem(), smem(), vmem(), vmem(), vmem()],
        out_specs=(vmem(), vmem()),
        scratch_shapes=[pltpu.VMEM((8, M), F32)],
        compiler_params=pltpu.CompilerParams(vmem_limit_bytes=16 * MIB),
        name="prepare",
    )(block_map, primal_map, schur, loads, mask)


def invert_kernel(
    bm_ref, schur_ref, mask_ref, ah_ref, al_ref, xh_ref, xl_ref, x, col, rhs_h, rhs_l, panel
):
    source = face_sources(bm_ref)
    eye = lax.broadcasted_iota(jnp.int32, (BW, BW), 0) == lax.broadcasted_iota(
        jnp.int32, (BW, BW), 1
    )
    for f in range(NB):
        row_at = pl.multiple_of(source[f] * BW, BW)
        for h in range(NB):
            col_at = pl.multiple_of(source[h] * BW, BW)
            block = schur_ref[pl.ds(row_at, BW), pl.ds(col_at, BW)]
            if f == h:
                penalty = 0.1 * mask_ref[:, pl.ds(col_at, BW)].astype(F32)
                block = block + jnp.where(eye, penalty, 0.0)
            x[f * BW : (f + 1) * BW, h * BW : (h + 1) * BW] = block
            high, low = split(block)
            ah_ref[f * BW : (f + 1) * BW, h * BW : (h + 1) * BW] = high
            al_ref[f * BW : (f + 1) * BW, h * BW : (h + 1) * BW] = low

    def step(k, carry):
        at = pl.multiple_of(k * BW, BW)
        here = pl.ds(at, BW)
        inverse = dense_inverse(x[here, here], BW)
        inv_h, inv_l = split(inverse)
        row_h, row_l = split(x[here, :])
        both = jnp.concatenate([inv_h, inv_l], 1)
        p = dot(both, jnp.concatenate([row_h, row_h], 0)) + dot(
            both, jnp.concatenate([row_l, row_l], 0)
        )
        panel[...] = p
        panel[:, here] = inverse
        p_h, p_l = split(panel[...])
        rhs_h[0:BW, :] = p_h
        rhs_h[BW:, :] = p_h
        rhs_l[0:BW, :] = p_l
        rhs_l[BW:, :] = p_l
        col_h, col_l = split(x[:, here])
        col[:, 0:BW] = col_h
        col[:, BW:] = col_l
        x[:, here] = jnp.zeros((M, BW), F32)
        for n in range(4):
            cols = slice(n * 256, (n + 1) * 256)
            x[:, cols] = x[:, cols] - (
                dot(col[...], rhs_h[:, cols]) + dot(col[...], rhs_l[:, cols])
            )
        x[here, :] = panel[...]
        return carry

    lax.fori_loop(0, NB, step, 0)
    for f in range(NB):
        rows = slice(f * BW, (f + 1) * BW)
        high, low = split(x[rows, :])
        xh_ref[rows, :] = high
        xl_ref[rows, :] = low


def invert(block_map, schur, mask):
    big = jax.ShapeDtypeStruct((M, M), BF16)
    return pl.pallas_call(
        invert_kernel,
        out_shape=(big, big, big, big),
        in_specs=[smem(), vmem(), vmem()],
        out_specs=(vmem(), vmem(), vmem(), vmem()),
        scratch_shapes=[
            pltpu.VMEM((M, M), F32),
            pltpu.VMEM((M, 2 * BW), BF16),
            pltpu.VMEM((2 * BW, M), BF16),
            pltpu.VMEM((2 * BW, M), BF16),
            pltpu.VMEM((BW, M), F32),
        ],
        compiler_params=pltpu.CompilerParams(vmem_limit_bytes=40 * MIB),
        cost_estimate=pl.CostEstimate(
            flops=20_000_000_000, bytes_accessed=12 * MIB, transcendentals=0
        ),
        name="invert",
    )(block_map, schur, mask)


def product(value, high_ref, low_ref):
    high, low = split(value)
    both = dot(jnp.concatenate([high, low], 0), high_ref[...])
    return both[:R] + both[R:] + dot(high, low_ref[...])


def iterate_kernel(
    loads_ref, low_ref, high_ref, tiles_ref, ah_ref, al_ref, xh_ref, xl_ref,
    sol_ref, res_ref,
    face_out, face_in, avg, sum_g, sum_x, sum_z,
    face_send, face_recv, avg_send, avg_recv, g_send, g_recv, x_send, x_recv, z_send, z_recv,
):
    s = lax.axis_index("sub")
    g = lax.axis_index("grp")
    n_sub = lax.axis_size("sub")
    n_grp = lax.axis_size("grp")
    n_z = n_sub // X_DIM
    xi = lax.rem(s, X_DIM)
    zi = s // X_DIM
    left = lax.rem(s + n_sub - 1, n_sub)
    right = lax.rem(s + 1, n_sub)

    def grp_peer(d):
        return (s, lax.rem(g + d, n_grp))

    def x_peer(d):
        return (zi * X_DIM + lax.rem(xi + d, X_DIM), g)

    def z_peer(d):
        return (lax.rem(zi + d, n_z) * X_DIM + xi, g)

    partners = [(left, g), (right, g)]
    partners += [grp_peer(d) for d in range(1, n_grp)]
    partners += [x_peer(d) for d in range(1, X_DIM)]
    partners += [z_peer(d) for d in range(1, n_z)]
    barrier = pltpu.get_barrier_semaphore()
    for partner in partners:
        pl.semaphore_signal(barrier, inc=1, device_id=partner, device_id_type=MESH)

    started = []

    def gather_start(buf, e, send, recv, peer, count, mine):
        for d in range(1, count):
            copy = pltpu.make_async_remote_copy(
                src_ref=buf.at[e, mine], dst_ref=buf.at[e, mine],
                send_sem=send.at[e, d], recv_sem=recv.at[e, mine],
                device_id=peer(d), device_id_type=MESH,
            )
            copy.start()
            started.append(copy)

    def gather_wait(buf, e, send, recv, peer, count, mine):
        for d in range(1, count):
            other = lax.rem(mine + d, count)
            pltpu.make_async_remote_copy(
                src_ref=buf.at[e, other], dst_ref=buf.at[e, other],
                send_sem=send.at[e, d], recv_sem=recv.at[e, other],
                device_id=peer(d), device_id_type=MESH,
            ).wait_recv()

    stages = {
        "avg": (avg, avg_send, avg_recv, grp_peer, n_grp, g),
        "g": (sum_g, g_send, g_recv, grp_peer, n_grp, g),
        "x": (sum_x, x_send, x_recv, x_peer, X_DIM, xi),
        "z": (sum_z, z_send, z_recv, z_peer, n_z, zi),
    }

    def begin(stage, e, tile):
        buf, send, recv, peer, count, mine = stages[stage]
        buf[e, mine] = tile
        gather_start(buf, e, send, recv, peer, count, mine)

    def end(stage, e):
        buf, send, recv, peer, count, mine = stages[stage]
        gather_wait(buf, e, send, recv, peer, count, mine)
        return buf

    def total(stage, e):
        buf = end(stage, e)
        out = buf[e, 0]
        for d in range(1, buf.shape[1]):
            out = out + buf[e, d]
        return out

    def exchange_start(e, value):
        face_out[e, 0] = value[:, : M // 2]
        face_out[e, 1] = value[:, M // 2 :]
        for side, target in ((0, left), (1, right)):
            copy = pltpu.make_async_remote_copy(
                src_ref=face_out.at[e, side], dst_ref=face_in.at[e, 1 - side],
                send_sem=face_send.at[e, side], recv_sem=face_recv.at[e, 1 - side],
                device_id=(target, g), device_id_type=MESH,
            )
            copy.start()
            started.append(copy)

    def exchange_end(e):
        for side, target in ((0, left), (1, right)):
            pltpu.make_async_remote_copy(
                src_ref=face_out.at[e, side], dst_ref=face_in.at[e, 1 - side],
                send_sem=face_send.at[e, side], recv_sem=face_recv.at[e, 1 - side],
                device_id=(target, g), device_id_type=MESH,
            ).wait_recv()
        first = face_out[e, 0] + face_in[e, 0]
        second = face_out[e, 1] + face_in[e, 1]
        return jnp.concatenate([first, second], 1)

    blocks = (
        lax.broadcasted_iota(jnp.int32, (8, M), 1) // BW
        == lax.broadcasted_iota(jnp.int32, (8, M), 0)
    ).astype(F32)
    sub = lax.broadcasted_iota(jnp.int32, (8, BW), 0)
    ones = jnp.ones((8, M), F32)
    pad = jnp.zeros((8, BW - R), F32)

    def averages(w):
        t = dot_hi(blocks, w, ((1,), (1,))) * (1.0 / ROOT)
        return jnp.concatenate([t, pad], 1)

    def sums_of(u, v):
        t = dot_hi(ones, u * v, ((1,), (1,)))
        return jnp.concatenate([t, pad], 1)

    def per_row(line):
        tile = jnp.where(sub == 0, jnp.broadcast_to(line, (8, BW)), 0.0)
        wide = dot_hi(tile, jnp.ones((8, BW), F32), ((0,), (0,)))[:R]
        return jnp.concatenate([wide] * NB, 1)

    right_side = loads_ref[...] + jnp.concatenate([low_ref[...], high_ref[...]], 1)
    weighted = 0.5 * right_side
    tile = averages(weighted)
    pl.semaphore_wait(barrier, len(partners))
    begin("avg", 0, tile)

    contributions = tiles_ref[...].reshape(n_grp * 8, BW)
    primal_all = contributions[:, C : 2 * C]
    local_all = contributions[:, :C]
    coarse = dot_hi(primal_all, local_all, ((0,), (0,)))
    coarse = coarse + (
        lax.broadcasted_iota(jnp.int32, (C, C), 0) == lax.broadcasted_iota(jnp.int32, (C, C), 1)
    ).astype(F32)
    coarse_inverse = dense_inverse(
        jnp.concatenate([coarse, jnp.zeros((C, BW - C), F32)], 1), C
    )[:, :C]
    primal = tiles_ref[g][:, C : 2 * C]
    weights = dot_hi(dot_hi(primal, coarse_inverse, ((1,), (0,))), primal_all, ((1,), (1,)))

    def correction(e):
        gathered = end("avg", e)[e].reshape(n_grp * 8, BW)
        amounts = dot_hi(weights, gathered, ((1,), (0,))) * (1.0 / ROOT)
        return dot_hi(amounts[:, :R], blocks, ((0,), (0,)))

    solved = product(weighted, xh_ref, xl_ref)
    local_z = 0.5 * (solved + correction(0))
    exchange_start(0, local_z)
    rz = sums_of(right_side, local_z)
    z = exchange_end(0)

    prod = product(z, ah_ref, al_ref)
    exchange_start(1, prod)
    dp = sums_of(z, prod)
    begin("g", 0, jnp.where(sub == 0, rz, dp))
    image = exchange_end(1)

    half = 0.5 * image
    begin("avg", 1, averages(half))
    begin("x", 0, total("g", 0))
    solved_q = product(half, xh_ref, xl_ref)
    local_q = 0.5 * (solved_q + correction(1))
    exchange_start(2, local_q)
    begin("z", 0, total("x", 0))
    first = total("z", 0)
    rz0 = first[0:1]
    dp0 = first[1:2]
    alpha0 = rz0 / jnp.where(lax.broadcasted_iota(jnp.int32, (1, BW), 1) < R, dp0, 1.0)
    alpha0_rows = per_row(alpha0)
    residual = right_side - alpha0_rows * image
    rz = sums_of(residual, local_z - alpha0_rows * local_q)
    z1 = z - alpha0_rows * exchange_end(2)

    prod1 = product(z1, ah_ref, al_ref)
    exchange_start(3, prod1)
    zz = sums_of(z1, prod1)
    zd = sums_of(z1, prod)
    begin("g", 1, jnp.where(sub == 0, rz, jnp.where(sub == 1, zz, zd)))
    begin("x", 1, total("g", 1))
    image1 = exchange_end(3)
    begin("z", 1, total("x", 1))
    last = total("z", 1)
    valid = lax.broadcasted_iota(jnp.int32, (1, BW), 1) < R
    rz1 = last[0:1]
    beta = rz1 / jnp.where(valid, rz0, 1.0)
    energy = last[1:2] + 2.0 * beta * last[2:3] + beta * beta * dp0
    alpha1 = rz1 / jnp.where(valid, energy, 1.0)
    alpha1_rows = per_row(alpha1)
    beta_rows = per_row(beta)
    sol_ref[...] = alpha0_rows * z + alpha1_rows * (z1 + beta_rows * z)
    res_ref[...] = residual - alpha1_rows * (image1 + beta_rows * image)
    for copy in started:
        copy.wait_send()


def iterate(n_grp, n_sub, *args):
    n_z = n_sub // X_DIM
    out = jax.ShapeDtypeStruct((R, M), F32)
    dma = pltpu.SemaphoreType.DMA
    return pl.pallas_call(
        iterate_kernel,
        out_shape=(out, out),
        in_specs=[vmem()] * 8,
        out_specs=(vmem(), vmem()),
        scratch_shapes=[
            pltpu.VMEM((4, 2, R, M // 2), F32),
            pltpu.VMEM((4, 2, R, M // 2), F32),
            pltpu.VMEM((2, n_grp, 8, BW), F32),
            pltpu.VMEM((2, n_grp, 8, BW), F32),
            pltpu.VMEM((2, X_DIM, 8, BW), F32),
            pltpu.VMEM((2, n_z, 8, BW), F32),
            dma((4, 2)),
            dma((4, 2)),
            dma((2, n_grp)),
            dma((2, n_grp)),
            dma((2, n_grp)),
            dma((2, n_grp)),
            dma((2, X_DIM)),
            dma((2, X_DIM)),
            dma((2, n_z)),
            dma((2, n_z)),
        ],
        compiler_params=pltpu.CompilerParams(
            collective_id=0, has_side_effects=True, vmem_limit_bytes=40 * MIB
        ),
        cost_estimate=pl.CostEstimate(
            flops=2_000_000_000, bytes_accessed=10 * MIB, transcendentals=0
        ),
        name="iterate",
    )(*args)


def body(schur, loads, block_map, primal_map, disk_mask):
    n_sub = lax.axis_size("sub")
    n_grp = lax.axis_size("grp")
    block_map = block_map[0]
    matrix = schur[0, 0]
    mask = disk_mask[0]
    face, tile = prepare(block_map, primal_map[0], matrix, loads[0, 0], mask)
    forward = [(i, (i + 1) % n_sub) for i in range(n_sub)]
    backward = [(i, (i - 1) % n_sub) for i in range(n_sub)]
    from_left = lax.ppermute(face[:, M // 2 :], "sub", forward)
    from_right = lax.ppermute(face[:, : M // 2], "sub", backward)
    tiles = lax.all_gather(tile, "grp")
    a_high, a_low, x_high, x_low = invert(block_map, matrix, mask)
    sol, res = iterate(
        n_grp, n_sub, face, from_left, from_right, tiles, a_high, a_low, x_high, x_low
    )
    return sol[None, None], res[None, None]


def solution(mesh):
    in_specs = (
        P("sub", "grp", None, None),
        P("sub", "grp", None, None),
        P("sub", "grp", None),
        P("sub", "grp", None),
        P("sub", "grp", None),
    )
    out_specs = (P("sub", "grp", None, None), P("sub", "grp", None, None))
    return jax.shard_map(body, mesh=mesh, in_specs=in_specs, out_specs=out_specs, check_vma=False)
```

time: 825 us -> 175 us (0.21); the launches traced: 813 us -> 175 us
  blocking collectives: 359 us -> 14.2 us
  other arithmetic: 274 us -> 0 us
  Pallas kernels: 0 us -> 137 us
  matrix products: 72.2 us -> 0 us
  local copies, waits for them, and re-layouts: 49.8 us -> 6.57 us
  starting transfers between devices: 39.4 us -> 16.2 us
  waiting for transfers between devices: 10.9 us -> 0.01 us
    psum x5 -> x0, blocking collectives: 359 us -> none  [the longest x2 211 us: residual_sum(): return lax.psum(inner_local(first_vec, second_vec), ('sub', 'grp'))]
    another operation x39 -> x0, other arithmetic: 258 us -> none  [the longest x30 167 us: body(): factor = jnp.linalg.cholesky(shifted)]
    pallas_call x0 -> x3, Pallas kernels: none -> 137 us  [the longest x1 75.7 us: invert(): pl.pallas_call(invert_kernel, out_shape=(big, big, big, big), in_specs=[s...]
    another operation x78 -> x0, matrix products: 54.8 us -> none  [the longest x14 26.4 us: body(): factor = jnp.linalg.cholesky(shifted)]
    another operation x84 -> x0, local copies, waits for them, and re-layouts: 29.1 us -> none  [the longest x41 23.2 us: chol_apply(): lax.linalg.triangular_solve(factor, values, left_side=False, lower=True,...]
    ppermute x10 -> x2, starting transfers between devices: 39.4 us -> 16.2 us  [the longest x1 14.3 us: body(): from_right = lax.ppermute(face[:, :M // 2], 'sub', backward)]
    dot_general x17 -> x0, matrix products: 17.4 us -> none  [the longest x2 11.8 us: body(): product = jnp.dot(to_local(direction), shifted, precision=highest)]
    all_gather x0 -> x1, blocking collectives: none -> 14.2 us  [body(): tiles = lax.all_gather(tile, 'grp')]
  transfers between devices with their start and end apart: 10 -> 2, of which waited for: 4 -> 0; matrix products, arithmetic and copies ran while one was open for 41% -> 0% of each run, Pallas kernels for 0% -> 43%
where the time goes in v1:
time: 175 us
  Pallas kernels  137 us (78%)
  starting transfers between devices  16.2 us (9%)
  blocking collectives  14.2 us (8%)
  local copies, waits for them, and re-layouts  6.57 us (4%)
    pallas_call x1, Pallas kernels, invert(): pl.pallas_call(invert_kernel, out_shape=(big, big, big, big), in_specs=[s...  75.7 us
    pallas_call x1, Pallas kernels, iterate(): pl.pallas_call(iterate_kernel, out_shape=(out, out), in_specs=[vmem()] *...  60.2 us
    ppermute x1, starting transfers between devices, body(): from_right = lax.ppermute(face[:, :M // 2], 'sub', backward)  14.3 us
    all_gather x1, blocking collectives, body(): tiles = lax.all_gather(tile, 'grp')  14.2 us
    unnamed x16, local copies, waits for them, and re-layouts  6.54 us
  transfers between devices with their start and end apart: 2, of which 0 were waited for; matrix products, arithmetic and copies ran while one was open for 0% of the time, Pallas kernels for 43%

profile of v1, /device:TPU:1, one launch (start us, length us, event | category | flops | bytes accessed | tf_op | source)
XLA Modules:
  0.0 174.9 jit_solution(2957915993540028874)
XLA Ops:
  0.6 0.0 copy-start
  0.6 2.2 %copy-done = f32[1,1,1024,1024]{3,2,1,0:T(8,128)S(1)} copy-done((f32[1,1,1024,1024]{3,2,1,0:T(8,128)S(1)}, f32[1,1,1024,1024]{3,2,1,0:T(8,128)}, u32[]{:S(2)}) %copy-start) | copy-done | bytes 4194328
  2.8 0.0 copy-start.2
  2.8 0.9 copy-done.2
  3.8 0.0 copy-start.3
  3.8 0.7 copy-done.3
  4.5 0.0 copy-start.4
  4.5 0.7 copy-done.4
  5.1 0.0 copy-start.5
  5.1 0.7 copy-done.5
  5.8 0.0 copy-start.1
  5.8 0.0 copy-start.6
  5.8 1.2 prepare.1
  7.0 14.3 %collective-permute-start.1 = (f32[64,512]{1,0:T(8,128)S(1)}, f32[64,512]{1,0:T(8,128)S(1)}, u32[]{:S(2)}, u32[]{:S(2)}) collective-permute-start(f32[64,512]{1,0:T(8,128)S(1)} %get-tuple-element.18), channel_id=1, source_target_pairs={{0,504},{8,0},{16,8},{24,16},{32,24},{40,32},{48,40},{56,48},{64,5... | collective-permute-start | bytes 393224 | tf_op jit(solution)/shard_map/ppermute | solution.py:521
  21.3 1.9 %collective-permute-start = (f32[64,512]{1,0:T(8,128)S(1)}, f32[64,512]{1,0:T(8,128)S(1)}, u32[]{:S(2)}, u32[]{:S(2)}) collective-permute-start(f32[64,512]{1,0:T(8,128)S(1)} %get-tuple-element.19), channel_id=1, source_target_pairs={{0,8},{8,16},{16,24},{24,32},{32,40},{40,48},{48,56},{56,64},{64,7... | collective-permute-start | bytes 393224 | tf_op jit(solution)/shard_map/ppermute | solution.py:520
  23.2 0.0 copy-done.1
  23.2 0.0 copy-done.6
  23.3 75.7 %invert.1 = (bf16[1024,1024]{1,0:T(8,128)(2,1)S(1)}, bf16[1024,1024]{1,0:T(8,128)(2,1)S(1)}, bf16[1024,1024]{1,0:T(8,128)(2,1)S(1)}, bf16[1024,1024]{1,0:T(8,128)(2,1)S(1)}) custom-call(s32[1,8]{1,0:T(1,128)S(1)} %bitcast.18, f32[1024,1024]{1,0:T(8,128)S(1)} %bitcast.9, s32[1,1024]{1,0:T(1,128)S(1)} %bitcast.15), custom_call_target="tpu_custom_call" | custom-call | flops 20000000000 | bytes 12582912 | tf_op jit(solution)/shard_map/invert/pallas_call | solution.py:252
  99.0 14.2 %all-gather = f32[64,128]{1,0:T(8,128)S(1)} all-gather(f32[8,128]{1,0:T(8,128)S(1)} %get-tuple-element.11), channel_id=2, replica_groups=mesh['sub'=64,'grp'=8] {'grp'}, dimensions={0}, use_global_device_ids=true | all-gather | bytes 36864 | tf_op jit(solution)/shard_map/all_gather | solution.py:522
  113.2 0.0 collective-permute-done.1.high_ref
  113.2 0.0 collective-permute-done.low_ref
  113.3 60.2 %iterate.1 = (f32[64,1024]{1,0:T(8,128)S(1)}, f32[64,1024]{1,0:T(8,128)S(1)}) custom-call(f32[64,1024]{1,0:T(8,128)S(1)} %get-tuple-element.10.loads_ref, f32[64,512]{1,0:T(8,128)S(1)} %collective-permute-done.low_ref, f32[64,512]{1,0:T(8,128)S(1)} %collective-permute-done.1.high_ref, f32[8,8,128]{2,1,0:T(8,128)S(1)} %bitcast.13, ...), custom_call_target="tpu_custom_call" | custom-call | flops 2000000000 | bytes 10485760 | tf_op jit(solution)/shard_map/iterate/pallas_call | solution.py:478
  173.5 0.7 copy.9
  174.2 0.7 copy.10
  (1 shorter events, 0.0 us)
Async XLA Ops:
  0.6 2.2 %copy-start = (f32[1,1,1024,1024]{3,2,1,0:T(8,128)S(1)}, f32[1,1,1024,1024]{3,2,1,0:T(8,128)}, u32[]{:S(2)}) copy-start(f32[1,1,1024,1024]{3,2,1,0:T(8,128)} %param.5) | copy-start | bytes 12582916
  2.8 0.9 copy-start.2
  3.8 0.7 copy-start.3
  4.5 0.7 copy-start.4
  5.1 0.7 copy-start.5
  5.8 17.5 %copy-start.1 = (f32[1,1,1024,1024]{3,2,1,0:T(8,128)S(1)}, f32[1,1,1024,1024]{3,2,1,0:T(8,128)}, u32[]{:S(2)}) copy-start(f32[1,1,1024,1024]{3,2,1,0:T(8,128)} %param.5) | copy-start | bytes 12582916
  5.8 17.5 %copy-start.6 = (s32[1,1,8]{2,1,0:T(1,128)S(1)}, s32[1,1,8]{2,1,0:T(1,128)}, u32[]{:S(2)}) copy-start(s32[1,1,8]{2,1,0:T(1,128)} %param.7) | copy-start | bytes 100
  7.0 106.2 %collective-permute-start.1 = (f32[64,512]{1,0:T(8,128)S(1)}, f32[64,512]{1,0:T(8,128)S(1)}, u32[]{:S(2)}, u32[]{:S(2)}) collective-permute-start(f32[64,512]{1,0:T(8,128)S(1)} %get-tuple-element.18), channel_id=1, source_target_pairs={{0,504},{8,0},{16,8},{24,16},{32,24},{40,32},{48,40},{56,48},{64,5... | collective-permute-start | bytes 393224 | tf_op jit(solution)/shard_map/ppermute | solution.py:521
  21.3 91.9 %collective-permute-start = (f32[64,512]{1,0:T(8,128)S(1)}, f32[64,512]{1,0:T(8,128)S(1)}, u32[]{:S(2)}, u32[]{:S(2)}) collective-permute-start(f32[64,512]{1,0:T(8,128)S(1)} %get-tuple-element.19), channel_id=1, source_target_pairs={{0,8},{8,16},{16,24},{24,32},{32,40},{40,48},{48,56},{56,64},{64,7... | collective-permute-start | bytes 393224 | tf_op jit(solution)/shard_map/ppermute | solution.py:520

commit v2 on v1

--- a/solution.py
+++ b/solution.py
@@ -47,7 +47,6 @@
 
 def recip(a):
     r = pltpu.reciprocal(a, approx=True)
-    r = r * (2.0 - a * r)
     return r * (2.0 - a * r)
 
 
@@ -101,7 +100,8 @@
     return r
 
 
-def dense_inverse(x, n):
+def dense_inverse(x, n, beside=()):
+    beside = list(beside)
     groups = n // 8
     xs = [x[8 * i : 8 * i + 8, :] for i in range(groups)]
     lane = lax.broadcasted_iota(jnp.int32, (8, BW), 1)
@@ -137,6 +137,10 @@
                     y = y - cols[i][j] * p[j]
             new.append(y)
         xs = new
+        if beside:
+            beside.pop(0)()
+    for work in beside:
+        work()
     return jnp.concatenate(xs, 0)
 
 
@@ -191,7 +195,8 @@
 
 
 def invert_kernel(
-    bm_ref, schur_ref, mask_ref, ah_ref, al_ref, xh_ref, xl_ref, x, col, rhs_h, rhs_l, panel
+    bm_ref, schur_ref, mask_ref, ah_ref, al_ref, out_ref, col, last_ref,
+    x, rhs, panel, pivot, inv,
 ):
     source = face_sources(bm_ref)
     eye = lax.broadcasted_iota(jnp.int32, (BW, BW), 0) == lax.broadcasted_iota(
@@ -209,57 +214,94 @@
             high, low = split(block)
             ah_ref[f * BW : (f + 1) * BW, h * BW : (h + 1) * BW] = high
             al_ref[f * BW : (f + 1) * BW, h * BW : (h + 1) * BW] = low
+    x[M:, :] = jnp.zeros((BW, M + BW), F32)
+    x[:M, M:] = jnp.zeros((M, BW), F32)
+    inv[...] = jnp.zeros((BW, BW), F32)
+    pivot[...] = x[0:BW, 0:BW]
+
+    def at(k):
+        return pl.ds(pl.multiple_of(k * BW, BW), BW)
+
+    def four(value, axis):
+        high, low = split(value)
+        parts = [high, low, high, low] if axis == 1 else [high, high, low, low]
+        return jnp.concatenate(parts, axis)
+
+    def rest(here):
+        def rows():
+            inverse = inv[...]
+            panel[...] = dot(four(inverse, 1), four(x[here, :M], 0))
+            col[...] = four(x[:M, here], 1)
+            x[:, here] = jnp.zeros((M + BW, BW), F32)
+
+        def finish():
+            x[here, :M] = panel[...]
+            x[here, here] = inv[...]
+
+        def block(n):
+            cols = slice(n * 256, (n + 1) * 256)
+
+            def work():
+                x[:M, cols] = x[:M, cols] - dot(col[...], rhs[:, cols])
+
+            return work
+
+        def sides():
+            rhs[:, :M] = four(panel[...], 0)
+            rhs[:, here] = four(inv[...], 0)
+
+        return rows, sides, [block(n) for n in range(4)], finish
 
     def step(k, carry):
-        at = pl.multiple_of(k * BW, BW)
-        here = pl.ds(at, BW)
-        inverse = dense_inverse(x[here, here], BW)
-        inv_h, inv_l = split(inverse)
-        row_h, row_l = split(x[here, :])
-        both = jnp.concatenate([inv_h, inv_l], 1)
-        p = dot(both, jnp.concatenate([row_h, row_h], 0)) + dot(
-            both, jnp.concatenate([row_l, row_l], 0)
-        )
-        panel[...] = p
-        panel[:, here] = inverse
-        p_h, p_l = split(panel[...])
-        rhs_h[0:BW, :] = p_h
-        rhs_h[BW:, :] = p_h
-        rhs_l[0:BW, :] = p_l
-        rhs_l[BW:, :] = p_l
-        col_h, col_l = split(x[:, here])
-        col[:, 0:BW] = col_h
-        col[:, BW:] = col_l
-        x[:, here] = jnp.zeros((M, BW), F32)
-        for n in range(4):
-            cols = slice(n * 256, (n + 1) * 256)
-            x[:, cols] = x[:, cols] - (
-                dot(col[...], rhs_h[:, cols]) + dot(col[...], rhs_l[:, cols])
-            )
-        x[here, :] = panel[...]
+        last = at(lax.rem(k + NB, NB + 1))
+        here = at(k)
+        after = at(jnp.minimum(k + 1, NB - 1))
+        rows, sides, blocks, finish = rest(last)
+        rows()
+        sides()
+
+        def nothing():
+            pass
+
+        work = []
+        for block in blocks:
+            work += [block, nothing, nothing]
+        inverse = dense_inverse(pivot[...], BW, work)
+        finish()
+        inv[...] = inverse
+        p = dot(four(inverse, 1), four(x[here, after], 0))
+        pivot[...] = x[after, after] - dot(four(x[after, here], 1), four(p, 0))
         return carry
 
     lax.fori_loop(0, NB, step, 0)
-    for f in range(NB):
-        rows = slice(f * BW, (f + 1) * BW)
-        high, low = split(x[rows, :])
-        xh_ref[rows, :] = high
-        xl_ref[rows, :] = low
+    rows, sides, blocks, finish = rest(at(NB - 1))
+    rows()
+    sides()
+    finish()
+    col[M - BW :, :] = jnp.zeros((BW, 4 * BW), BF16)
+    last_ref[...] = rhs[:, :M]
+    out_ref[...] = x[:M, :M]
 
 
 def invert(block_map, schur, mask):
     big = jax.ShapeDtypeStruct((M, M), BF16)
     return pl.pallas_call(
         invert_kernel,
-        out_shape=(big, big, big, big),
+        out_shape=(
+            big,
+            big,
+            jax.ShapeDtypeStruct((M, M), F32),
+            jax.ShapeDtypeStruct((M, 4 * BW), BF16),
+            jax.ShapeDtypeStruct((4 * BW, M), BF16),
+        ),
         in_specs=[smem(), vmem(), vmem()],
-        out_specs=(vmem(), vmem(), vmem(), vmem()),
+        out_specs=(vmem(),) * 5,
         scratch_shapes=[
-            pltpu.VMEM((M, M), F32),
-            pltpu.VMEM((M, 2 * BW), BF16),
-            pltpu.VMEM((2 * BW, M), BF16),
-            pltpu.VMEM((2 * BW, M), BF16),
+            pltpu.VMEM((M + BW, M + BW), F32),
+            pltpu.VMEM((4 * BW, M + BW), BF16),
             pltpu.VMEM((BW, M), F32),
+            pltpu.VMEM((BW, BW), F32),
+            pltpu.VMEM((BW, BW), F32),
         ],
         compiler_params=pltpu.CompilerParams(vmem_limit_bytes=40 * MIB),
         cost_estimate=pl.CostEstimate(
@@ -276,9 +318,9 @@
 
 
 def iterate_kernel(
-    loads_ref, low_ref, high_ref, tiles_ref, ah_ref, al_ref, xh_ref, xl_ref,
+    loads_ref, tile_ref, ah_ref, al_ref, x_ref, col_ref, rhs_ref,
     sol_ref, res_ref,
-    face_out, face_in, avg, sum_g, sum_x, sum_z,
+    xh_ref, xl_ref, face_out, face_in, avg, sum_g, sum_x, sum_z,
     face_send, face_recv, avg_send, avg_recv, g_send, g_recv, x_send, x_recv, z_send, z_recv,
 ):
     s = lax.axis_index("sub")
@@ -397,13 +439,23 @@
         wide = dot_hi(tile, jnp.ones((8, BW), F32), ((0,), (0,)))[:R]
         return jnp.concatenate([wide] * NB, 1)
 
-    right_side = loads_ref[...] + jnp.concatenate([low_ref[...], high_ref[...]], 1)
+    def last_product(n):
+        cols = slice(n * 256, (n + 1) * 256)
+        xh_ref[:, cols], xl_ref[:, cols] = split(
+            x_ref[:, cols] - dot(col_ref[...], rhs_ref[:, cols])
+        )
+
+    last_product(0)
+    pl.semaphore_wait(barrier, len(partners))
+    begin("avg", 2, tile_ref[...])
+    exchange_start(4, loads_ref[...])
+    for n in range(1, 4):
+        last_product(n)
+    right_side = exchange_end(4)
     weighted = 0.5 * right_side
-    tile = averages(weighted)
-    pl.semaphore_wait(barrier, len(partners))
-    begin("avg", 0, tile)
-
-    contributions = tiles_ref[...].reshape(n_grp * 8, BW)
+    begin("avg", 0, averages(weighted))
+
+    contributions = end("avg", 2)[2].reshape(n_grp * 8, BW)
     primal_all = contributions[:, C : 2 * C]
     local_all = contributions[:, :C]
     coarse = dot_hi(primal_all, local_all, ((0,), (0,)))
@@ -413,7 +465,7 @@
     coarse_inverse = dense_inverse(
         jnp.concatenate([coarse, jnp.zeros((C, BW - C), F32)], 1), C
     )[:, :C]
-    primal = tiles_ref[g][:, C : 2 * C]
+    primal = tile_ref[:, C : 2 * C]
     weights = dot_hi(dot_hi(primal, coarse_inverse, ((1,), (0,))), primal_all, ((1,), (1,)))
 
     def correction(e):
@@ -478,19 +530,21 @@
     return pl.pallas_call(
         iterate_kernel,
         out_shape=(out, out),
-        in_specs=[vmem()] * 8,
+        in_specs=[vmem()] * 7,
         out_specs=(vmem(), vmem()),
         scratch_shapes=[
-            pltpu.VMEM((4, 2, R, M // 2), F32),
-            pltpu.VMEM((4, 2, R, M // 2), F32),
-            pltpu.VMEM((2, n_grp, 8, BW), F32),
+            pltpu.VMEM((M, M), BF16),
+            pltpu.VMEM((M, M), BF16),
+            pltpu.VMEM((5, 2, R, M // 2), F32),
+            pltpu.VMEM((5, 2, R, M // 2), F32),
+            pltpu.VMEM((3, n_grp, 8, BW), F32),
             pltpu.VMEM((2, n_grp, 8, BW), F32),
             pltpu.VMEM((2, X_DIM, 8, BW), F32),
             pltpu.VMEM((2, n_z, 8, BW), F32),
-            dma((4, 2)),
-            dma((4, 2)),
-            dma((2, n_grp)),
-            dma((2, n_grp)),
+            dma((5, 2)),
+            dma((5, 2)),
+            dma((3, n_grp)),
+            dma((3, n_grp)),
             dma((2, n_grp)),
             dma((2, n_grp)),
             dma((2, X_DIM)),
@@ -515,15 +569,8 @@
     matrix = schur[0, 0]
     mask = disk_mask[0]
     face, tile = prepare(block_map, primal_map[0], matrix, loads[0, 0], mask)
-    forward = [(i, (i + 1) % n_sub) for i in range(n_sub)]
-    backward = [(i, (i - 1) % n_sub) for i in range(n_sub)]
-    from_left = lax.ppermute(face[:, M // 2 :], "sub", forward)
-    from_right = lax.ppermute(face[:, : M // 2], "sub", backward)
-    tiles = lax.all_gather(tile, "grp")
-    a_high, a_low, x_high, x_low = invert(block_map, matrix, mask)
-    sol, res = iterate(
-        n_grp, n_sub, face, from_left, from_right, tiles, a_high, a_low, x_high, x_low
-    )
+    a_high, a_low, x_part, col, rhs = invert(block_map, matrix, mask)
+    sol, res = iterate(n_grp, n_sub, face, tile, a_high, a_low, x_part, col, rhs)
     return sol[None, None], res[None, None]
 
 

time: 175 us -> 132 us (0.75)
  starting transfers between devices: 16.2 us -> 0 us
  blocking collectives: 14.2 us -> 0 us
  Pallas kernels: 137 us -> 125 us
    pallas_call x1, Pallas kernels: 75.7 us -> 50.1 us  [invert(): pl.pallas_call(invert_kernel, out_shape=(big, big, jax.ShapeDtypeStruct((...]
    ppermute x2 -> x0, starting transfers between devices: 16.2 us -> none  [the longest x1 14.3 us: body(): from_right = lax.ppermute(face[:, :M // 2], 'sub', backward)]
    all_gather x1 -> x0, blocking collectives: 14.2 us -> none  [body(): tiles = lax.all_gather(tile, 'grp')]
    pallas_call x1, Pallas kernels: 60.2 us -> 73.5 us  [iterate(): pl.pallas_call(iterate_kernel, out_shape=(out, out), in_specs=[vmem()] *...]
  transfers between devices with their start and end apart: 2 -> 0, of which waited for: 0 -> 0; matrix products, arithmetic and copies ran while one was open for 0% -> 0% of each run, Pallas kernels for 43% -> 0%
where the time goes in v2:
time: 132 us
  Pallas kernels  125 us (95%)
  local copies, waits for them, and re-layouts  6.55 us (5%)
    pallas_call x1, Pallas kernels, iterate(): pl.pallas_call(iterate_kernel, out_shape=(out, out), in_specs=[vmem()] *...  73.5 us
    pallas_call x1, Pallas kernels, invert(): pl.pallas_call(invert_kernel, out_shape=(big, big, jax.ShapeDtypeStruct((...  50.1 us
    unnamed x16, local copies, waits for them, and re-layouts  6.55 us

profile of v2, /device:TPU:1, one launch (start us, length us, event | category | flops | bytes accessed | tf_op | source)
XLA Modules:
  0.0 132.1 jit_solution(5217244366898990686)
XLA Ops:
  0.6 0.0 copy-start.3
  0.6 0.0 copy-start.6
  0.7 0.0 copy-start
  0.7 2.2 %copy-done = f32[1,1,1024,1024]{3,2,1,0:T(8,128)S(1)} copy-done((f32[1,1,1024,1024]{3,2,1,0:T(8,128)S(1)}, f32[1,1,1024,1024]{3,2,1,0:T(8,128)}, u32[]{:S(2)}) %copy-start) | copy-done | bytes 4194328
  2.9 0.0 copy-start.1
  2.9 0.9 copy-done.1
  3.8 0.0 copy-start.2
  3.8 0.7 copy-done.2
  4.5 0.0 copy-start.4
  4.5 0.7 copy-done.4
  5.1 0.0 copy-start.5
  5.1 0.7 copy-done.5
  5.8 1.2 prepare.1
  7.0 0.0 copy-done.3
  7.0 0.0 copy-done.6
  7.0 50.1 %invert.1 = (bf16[1024,1024]{1,0:T(8,128)(2,1)S(1)}, bf16[1024,1024]{1,0:T(8,128)(2,1)S(1)}, f32[1024,1024]{1,0:T(8,128)S(1)}, bf16[1024,512]{1,0:T(8,128)(2,1)S(1)}, bf16[512,1024]{1,0:T(8,128)(2,1)S(1)}) custom-call(s32[1,8]{1,0:T(1,128)S(1)} %bitcast.16, f32[1024,1024]{1,0:T(8,128)} %bitcast.7, s32[1,1024]{1,0:T(1,128)S(1)} %bitcast.13), custom_call_target="tpu_custom_call" | custom-call | flops 20000000000 | bytes 12582912 | tf_op jit(solution)/shard_map/invert/pallas_call | solution.py:288
  57.1 73.5 %iterate.1 = (f32[64,1024]{1,0:T(8,128)S(1)}, f32[64,1024]{1,0:T(8,128)S(1)}) custom-call(f32[64,1024]{1,0:T(8,128)S(1)} %get-tuple-element.11.loads_ref, f32[8,128]{1,0:T(8,128)S(1)} %get-tuple-element.12.tile_ref, bf16[1024,1024]{1,0:T(8,128)(2,1)S(1)} %get-tuple-element.13.ah_ref, bf16[1024,1024]{1,0:T(8,128)(2,1)S(1)} %get-tuple-element.14.al_ref, ...), custom_call_target="tpu_custom_call" | custom-call | flops 2000000000 | bytes 10485760 | tf_op jit(solution)/shard_map/iterate/pallas_call | solution.py:530
  130.6 0.7 copy.9
  131.4 0.7 copy.10
Async XLA Ops:
  0.6 6.4 %copy-start.3 = (s32[1,1,1024]{2,1,0:T(1,128)S(1)}, s32[1,1,1024]{2,1,0:T(1,128)}, u32[]{:S(2)}) copy-start(s32[1,1,1024]{2,1,0:T(1,128)} %param.9) | copy-start | bytes 12292
  0.6 6.4 %copy-start.6 = (s32[1,1,8]{2,1,0:T(1,128)S(1)}, s32[1,1,8]{2,1,0:T(1,128)}, u32[]{:S(2)}) copy-start(s32[1,1,8]{2,1,0:T(1,128)} %param.7) | copy-start | bytes 100
  0.7 2.2 %copy-start = (f32[1,1,1024,1024]{3,2,1,0:T(8,128)S(1)}, f32[1,1,1024,1024]{3,2,1,0:T(8,128)}, u32[]{:S(2)}) copy-start(f32[1,1,1024,1024]{3,2,1,0:T(8,128)} %param.5) | copy-start | bytes 12582916
  2.9 0.9 copy-start.1
  3.8 0.7 copy-start.2
  4.5 0.7 copy-start.4
  5.1 0.7 copy-start.5

commit v3 on v2

v3 whole, which is shorter than its diff:
```python
import jax
import jax.numpy as jnp
from jax import lax
from jax.experimental import pallas as pl
from jax.experimental.pallas import tpu as pltpu
from jax.sharding import PartitionSpec as P

F32 = jnp.float32
BF16 = jnp.bfloat16
HI = lax.Precision.HIGHEST
MESH = pl.DeviceIdType.MESH
M = 1024
R = 64
BW = 128
NB = 8
C = 32
X_DIM = 4
FIRST = NB - 2
ROOT = BW ** 0.5
MIB = 1 << 20


def vmem():
    return pl.BlockSpec(memory_space=pltpu.VMEM)


def smem():
    return pl.BlockSpec(memory_space=pltpu.SMEM)


def split(value):
    high = value.astype(BF16)
    low = (value - high.astype(F32)).astype(BF16)
    return high, low


def dot(a, b):
    return jnp.dot(a, b, preferred_element_type=F32)


def dot_hi(a, b, dims):
    return lax.dot_general(a, b, (dims, ((), ())), precision=HI, preferred_element_type=F32)


def spread(v):
    return jnp.broadcast_to(v, (8, BW))


def recip(a):
    r = pltpu.reciprocal(a, approx=True)
    return r * (2.0 - a * r)


def small_mm(a, b):
    out = []
    for i in range(len(a)):
        row = []
        for j in range(len(b[0])):
            t = a[i][0] * b[0][j]
            for l in range(1, len(b)):
                t = t + a[i][l] * b[l][j]
            row.append(t)
        out.append(row)
    return out


def small_inverse(d):
    n = len(d)
    if n == 2:
        a, b, e = d[0][0], d[0][1], d[1][1]
        r = recip(a * e - b * b)
        o = -(b * r)
        return [[e * r, o], [o, a * r]]
    h = n // 2
    a = small_inverse([row[:h] for row in d[:h]])
    b = [row[h:] for row in d[:h]]
    t = small_mm(a, b)
    s = [[None] * h for _ in range(h)]
    for i in range(h):
        for j in range(i, h):
            u = b[0][i] * t[0][j]
            for l in range(1, h):
                u = u + b[l][i] * t[l][j]
            s[i][j] = d[h + i][h + j] - u
            s[j][i] = s[i][j]
    s = small_inverse(s)
    ts = small_mm(t, s)
    r = [[None] * n for _ in range(n)]
    for i in range(h):
        for j in range(h):
            r[h + i][h + j] = s[i][j]
            r[i][h + j] = -ts[i][j]
            r[h + j][i] = r[i][h + j]
    for i in range(h):
        for j in range(i, h):
            u = a[i][j]
            for l in range(h):
                u = u + ts[i][l] * t[j][l]
            r[i][j] = u
            r[j][i] = u
    return r


def dense_inverse(x, n, beside=()):
    beside = list(beside)
    groups = n // 8
    xs = [x[8 * i : 8 * i + 8, :] for i in range(groups)]
    lane = lax.broadcasted_iota(jnp.int32, (8, BW), 1)
    sub = lax.broadcasted_iota(jnp.int32, (8, BW), 0)
    for q in range(groups):
        k = 8 * q
        rows = [spread(xs[q][j : j + 1, :]) for j in range(8)]
        d = [[None] * 8 for _ in range(8)]
        for i in range(8):
            for j in range(i, 8):
                d[i][j] = spread(rows[i][:, k + j : k + j + 1])
                d[j][i] = d[i][j]
        cols = [[spread(xs[i][:, k + j : k + j + 1]) for j in range(8)] for i in range(groups)]
        r = small_inverse(d)
        p = []
        for i in range(8):
            u = r[i][0] * rows[0]
            for j in range(1, 8):
                u = u + r[i][j] * rows[j]
            for j in range(8):
                u = jnp.where(lane == k + j, r[i][j], u)
            p.append(u)
        pivots = (lane >= k) & (lane < k + 8)
        new = []
        for i in range(groups):
            if i == q:
                y = p[0]
                for j in range(1, 8):
                    y = jnp.where(sub == j, p[j], y)
            else:
                y = jnp.where(pivots, 0.0, xs[i])
                for j in range(8):
                    y = y - cols[i][j] * p[j]
            new.append(y)
        xs = new
        if beside:
            beside.pop(0)()
    for work in beside:
        work()
    return jnp.concatenate(xs, 0)


def face_sources(bm_ref):
    places = [bm_ref[0, j] for j in range(NB)]
    out = []
    for f in range(NB):
        where = jnp.int32(0)
        for j in range(NB):
            where = where + jnp.where(places[j] == f, jnp.int32(j), jnp.int32(0))
        out.append(where)
    return out


def at(k):
    return pl.ds(pl.multiple_of(k * BW, BW), BW)


def four(value, axis):
    high, low = split(value)
    parts = [high, low, high, low] if axis == 1 else [high, high, low, low]
    return jnp.concatenate(parts, axis)


def elimination(x, col, rhs, panel, inv, here):
    def rows():
        panel[...] = dot(four(inv[...], 1), four(x[here, :M], 0))
        col[...] = four(x[:M, here], 1)
        x[:, here] = jnp.zeros((x.shape[0], BW), F32)
        rhs[:, :M] = four(panel[...], 0)
        rhs[:, here] = four(inv[...], 0)

    def block(n):
        cols = slice(n * 256, (n + 1) * 256)

        def work():
            x[:M, cols] = x[:M, cols] - dot(col[...], rhs[:, cols])

        return work

    def finish():
        x[here, :M] = panel[...]
        x[here, here] = inv[...]

    return rows, [block(n) for n in range(4)], finish


def nothing():
    pass


def pivot_step(x, col, rhs, panel, inv, pivot, last, here, after):
    rows, blocks, finish = elimination(x, col, rhs, panel, inv, last)
    rows()
    work = []
    for block in blocks:
        work += [block, nothing, nothing]
    inverse = dense_inverse(pivot[...], BW, work)
    finish()
    inv[...] = inverse
    if after is not None:
        p = dot(four(inverse, 1), four(x[here, after], 0))
        pivot[...] = x[after, after] - dot(four(x[after, here], 1), four(p, 0))


def invert_kernel(
    bm_ref, pm_ref, schur_ref, loads_ref, mask_ref,
    ah_ref, al_ref, x, inv, pivot, face_ref, tile_ref,
    col, rhs, panel, sums,
):
    source = face_sources(bm_ref)
    eye = lax.broadcasted_iota(jnp.int32, (BW, BW), 0) == lax.broadcasted_iota(
        jnp.int32, (BW, BW), 1
    )
    for f in range(NB):
        row_at = pl.multiple_of(source[f] * BW, BW)
        face_ref[:, f * BW : (f + 1) * BW] = loads_ref[:, pl.ds(row_at, BW)]
        for h in range(NB):
            col_at = pl.multiple_of(source[h] * BW, BW)
            block = schur_ref[pl.ds(row_at, BW), pl.ds(col_at, BW)]
            if f == h:
                penalty = 0.1 * mask_ref[:, pl.ds(col_at, BW)].astype(F32)
                block = block + jnp.where(eye, penalty, 0.0)
            x[f * BW : (f + 1) * BW, h * BW : (h + 1) * BW] = block
            sums[f : f + 1, h * BW : (h + 1) * BW] = jnp.sum(block, axis=0, keepdims=True)
            high, low = split(block)
            ah_ref[f * BW : (f + 1) * BW, h * BW : (h + 1) * BW] = high
            al_ref[f * BW : (f + 1) * BW, h * BW : (h + 1) * BW] = low
    x[M:, :] = jnp.zeros((BW, M + BW), F32)
    x[:M, M:] = jnp.zeros((M, BW), F32)
    inv[...] = jnp.zeros((BW, BW), F32)
    pivot[...] = x[0:BW, 0:BW]

    sub = lax.broadcasted_iota(jnp.int32, (8, BW), 0)
    lane = lax.broadcasted_iota(jnp.int32, (8, BW), 1)
    primal = jnp.zeros((8, BW), F32)
    shifted = jnp.zeros((8, BW), F32)
    for f in range(NB):
        coarse = pm_ref[0, source[f]]
        primal = jnp.where((sub == f) & (lane == coarse), 1.0, primal)
        shifted = jnp.where((sub == f) & (lane == coarse + C), 1.0, shifted)
    block_sums = dot_hi(sums[...], block_indicator(), ((1,), (1,))) / BW
    tile_ref[...] = dot_hi(block_sums, primal, ((1,), (0,))) + shifted

    def step(k, carry):
        last = at(lax.rem(k + NB, NB + 1))
        pivot_step(x, col, rhs, panel, inv, pivot, last, at(k), at(k + 1))
        return carry

    lax.fori_loop(0, FIRST, step, 0)


def invert(block_map, primal_map, schur, loads, mask):
    def arr(shape, dtype=F32):
        return jax.ShapeDtypeStruct(shape, dtype)

    return pl.pallas_call(
        invert_kernel,
        out_shape=(
            arr((M, M), BF16), arr((M, M), BF16), arr((M + BW, M + BW)), arr((BW, BW)),
            arr((BW, BW)), arr((R, M)), arr((8, BW)),
        ),
        in_specs=[smem(), smem(), vmem(), vmem(), vmem()],
        out_specs=(vmem(),) * 7,
        scratch_shapes=[
            pltpu.VMEM((M, 4 * BW), BF16),
            pltpu.VMEM((4 * BW, M + BW), BF16),
            pltpu.VMEM((BW, M), F32),
            pltpu.VMEM((8, M), F32),
        ],
        compiler_params=pltpu.CompilerParams(vmem_limit_bytes=40 * MIB),
        cost_estimate=pl.CostEstimate(
            flops=20_000_000_000, bytes_accessed=12 * MIB, transcendentals=0
        ),
        name="invert",
    )(block_map, primal_map, schur, loads, mask)


def block_indicator():
    return (
        lax.broadcasted_iota(jnp.int32, (8, M), 1) // BW
        == lax.broadcasted_iota(jnp.int32, (8, M), 0)
    ).astype(F32)


def product(value, high_ref, low_ref):
    high, low = split(value)
    both = dot(jnp.concatenate([high, low], 0), high_ref[...])
    return both[:R] + both[R:] + dot(high, low_ref[...])


def iterate_kernel(
    loads_ref, tile_ref, ah_ref, al_ref, x_ref, inv_ref, pivot_ref,
    sol_ref, res_ref,
    xh_ref, xl_ref, x, col, rhs, panel, inv, pivot,
    face_out, face_in, tiles, avg, weights_out, weights_in, sum_gx, sum_z,
    face_send, face_recv, tile_send, tile_recv, avg_send, avg_recv, w_send, w_recv,
    gx_send, gx_recv, z_send, z_recv,
):
    s = lax.axis_index("sub")
    g = lax.axis_index("grp")
    n_sub = lax.axis_size("sub")
    n_grp = lax.axis_size("grp")
    n_z = n_sub // X_DIM
    n_gx = n_grp * X_DIM
    xi = lax.rem(s, X_DIM)
    zi = s // X_DIM
    left = lax.rem(s + n_sub - 1, n_sub)
    right = lax.rem(s + 1, n_sub)
    mine = xi * n_grp + g

    def around(d):
        return lax.rem(g + d, n_grp)

    def gx_peer(d):
        return (zi * X_DIM + lax.rem(xi + d // n_grp, X_DIM), around(d % n_grp))

    def gx_slot(d):
        return lax.rem(xi + d // n_grp, X_DIM) * n_grp + around(d % n_grp)

    def z_peer(d):
        return (lax.rem(zi + d, n_z) * X_DIM + xi, g)

    partners = [(left, around(d)) for d in range(n_grp)]
    partners += [(right, around(d)) for d in range(n_grp)]
    partners += [gx_peer(d) for d in range(1, n_gx)]
    partners += [z_peer(d) for d in range(1, n_z)]
    barrier = pltpu.get_barrier_semaphore()
    for partner in partners:
        pl.semaphore_signal(barrier, inc=1, device_id=partner, device_id_type=MESH)

    started = []

    def copy_of(src, dst, send, recv, target):
        return pltpu.make_async_remote_copy(
            src_ref=src, dst_ref=dst, send_sem=send, recv_sem=recv,
            device_id=target, device_id_type=MESH,
        )

    def start(*args):
        copy = copy_of(*args)
        copy.start()
        started.append(copy)

    def wait(*args):
        copy_of(*args).wait_recv()

    def gx_begin(e, tile):
        sum_gx[e, mine] = tile
        for d in range(1, n_gx):
            start(
                sum_gx.at[e, mine], sum_gx.at[e, mine],
                gx_send.at[e, d], gx_recv.at[e, mine], gx_peer(d),
            )

    def gx_total(e):
        for d in range(1, n_gx):
            o = gx_slot(d)
            wait(sum_gx.at[e, o], sum_gx.at[e, o], gx_send.at[e, d], gx_recv.at[e, o], gx_peer(d))
        return jnp.sum(sum_gx[e], axis=0)

    def z_begin(e, tile):
        sum_z[e, zi] = tile
        for d in range(1, n_z):
            start(
                sum_z.at[e, zi], sum_z.at[e, zi], z_send.at[e, d], z_recv.at[e, zi], z_peer(d)
            )

    def z_total(e):
        for d in range(1, n_z):
            o = lax.rem(zi + d, n_z)
            wait(sum_z.at[e, o], sum_z.at[e, o], z_send.at[e, d], z_recv.at[e, o], z_peer(d))
        return jnp.sum(sum_z[e], axis=0)

    def avg_begin(e, tile):
        avg[e, 0, g] = tile
        for d in range(1, n_grp):
            start(
                avg.at[e, 0, g], avg.at[e, 0, g],
                avg_send.at[e, 0, d], avg_recv.at[e, 0, g], (s, around(d)),
            )
        for side, target in ((1, right), (2, left)):
            for d in range(n_grp):
                start(
                    avg.at[e, 0, g], avg.at[e, side, g],
                    avg_send.at[e, side, d], avg_recv.at[e, side, g], (target, around(d)),
                )

    def avg_end(e):
        for side, target in ((0, s), (1, right), (2, left)):
            for d in range(0 if side else 1, n_grp):
                o = around(d)
                wait(
                    avg.at[e, side, o], avg.at[e, side, o],
                    avg_send.at[e, side, d], avg_recv.at[e, side, o], (target, o),
                )

    def face_args(e, side):
        return (
            face_out.at[e, side], face_in.at[e, 1 - side],
            face_send.at[e, side], face_recv.at[e, 1 - side],
            ((left, right)[side], g),
        )

    def exchange_start(e, value):
        face_out[e, 0] = value[:, : M // 2]
        face_out[e, 1] = value[:, M // 2 :]
        for side in range(2):
            start(*face_args(e, side))

    def exchange_end(e):
        for side in range(2):
            wait(*face_args(e, side))
        first = face_out[e, 0] + face_in[e, 0]
        second = face_out[e, 1] + face_in[e, 1]
        return jnp.concatenate([first, second], 1)

    blocks = block_indicator()
    sub = lax.broadcasted_iota(jnp.int32, (8, BW), 0)
    ones = jnp.ones((8, M), F32)
    pad = jnp.zeros((8, BW - R), F32)

    def averages(w):
        t = dot_hi(blocks, w, ((1,), (1,))) * (1.0 / ROOT)
        return jnp.concatenate([t, pad], 1)

    def sums_of(u, v):
        t = dot_hi(ones, u * v, ((1,), (1,)))
        return jnp.concatenate([t, pad], 1)

    def per_row(line):
        tile = jnp.where(sub == 0, jnp.broadcast_to(line, (8, BW)), 0.0)
        wide = dot_hi(tile, jnp.ones((8, BW), F32), ((0,), (0,)))[:R]
        return jnp.concatenate([wide] * NB, 1)

    def piece(k):
        return slice(k * BW, (k + 1) * BW)

    x[...] = x_ref[:M, :M]
    inv[...] = inv_ref[...]
    pivot[...] = pivot_ref[...]
    pivot_step(
        x, col, rhs, panel, inv, pivot, piece(NB - 3), piece(NB - 2), piece(NB - 1)
    )
    pl.semaphore_wait(barrier, len(partners))
    tiles[g] = tile_ref[...]
    for d in range(1, n_grp):
        start(tiles.at[g], tiles.at[g], tile_send.at[d], tile_recv.at[g], (s, around(d)))
    exchange_start(4, loads_ref[...])
    pivot_step(x, col, rhs, panel, inv, pivot, piece(NB - 2), piece(NB - 1), None)
    rows, _, finish = elimination(x, col, rhs, panel, inv, piece(NB - 1))
    rows()
    finish()
    col[M - BW :, :] = jnp.zeros((BW, 4 * BW), BF16)

    for d in range(1, n_grp):
        o = around(d)
        wait(tiles.at[o], tiles.at[o], tile_send.at[d], tile_recv.at[o], (s, o))
    contributions = tiles[...].reshape(n_grp * 8, BW)
    primal_all = contributions[:, C : 2 * C]
    local_all = contributions[:, :C]
    coarse = dot_hi(primal_all, local_all, ((0,), (0,)))
    coarse = coarse + (
        lax.broadcasted_iota(jnp.int32, (C, C), 0) == lax.broadcasted_iota(jnp.int32, (C, C), 1)
    ).astype(F32)
    coarse_inverse = dense_inverse(
        jnp.concatenate([coarse, jnp.zeros((C, BW - C), F32)], 1), C
    )[:, :C]
    primal = tile_ref[:, C : 2 * C]
    weights = dot_hi(dot_hi(primal, coarse_inverse, ((1,), (0,))), primal_all, ((1,), (1,)))
    for n in range(4):
        cols = slice(n * 256, (n + 1) * 256)
        xh_ref[:, cols], xl_ref[:, cols] = split(x[:, cols] - dot(col[...], rhs[:, cols]))

    def weight_args(side):
        return (
            weights_out, weights_in.at[1 - side], w_send.at[side], w_recv.at[1 - side],
            ((left, right)[side], g),
        )

    weights_out[...] = jnp.concatenate([weights, jnp.zeros((8, BW - n_grp * 8), F32)], 1)
    for side in range(2):
        start(*weight_args(side))

    def amounts(e):
        avg_end(e)
        part = [
            dot_hi(w, avg[e, side].reshape(n_grp * 8, BW), ((1,), (0,))) * (1.0 / ROOT)
            for side, w in enumerate(weight_sides)
        ]
        return part[0], part[0] + part[1] + part[2]

    def expand(tile):
        return dot_hi(tile[:, :R], blocks, ((0,), (0,)))

    right_side = exchange_end(4)
    weighted = 0.5 * right_side
    mean = averages(weighted)
    avg_begin(0, mean)

    local_z = 0.5 * product(weighted, xh_ref, xl_ref)
    exchange_start(0, local_z)
    for side in range(2):
        wait(*weight_args(side))
    swapped = [pltpu.roll(weights_in[side], 4, 0)[:, : n_grp * 8] for side in range(2)]
    upper = lax.broadcasted_iota(jnp.int32, (8, n_grp * 8), 0) < 4
    weight_sides = [
        weights,
        jnp.where(upper, swapped[0], 0.0),
        jnp.where(upper, 0.0, swapped[1]),
    ]
    own, both = amounts(0)
    rz = sums_of(right_side, local_z) + ROOT * jnp.sum(own * mean, axis=0, keepdims=True)
    coarse_z = 0.5 * expand(both)
    z = exchange_end(0) + coarse_z

    prod = product(z, ah_ref, al_ref)
    exchange_start(1, prod)
    dp = sums_of(z, prod)
    gx_begin(0, jnp.where(sub == 0, rz, dp))
    image = exchange_end(1)

    half = 0.5 * image
    mean_q = averages(half)
    avg_begin(1, mean_q)
    local_q = 0.5 * product(half, xh_ref, xl_ref)
    exchange_start(2, local_q)
    z_begin(0, gx_total(0))
    own_q, both_q = amounts(1)
    coarse_q = 0.5 * expand(both_q)
    q = exchange_end(2) + coarse_q
    first = z_total(0)
    valid = lax.broadcasted_iota(jnp.int32, (1, BW), 1) < R
    rz0 = first[0:1]
    dp0 = first[1:2]
    alpha0 = rz0 / jnp.where(valid, dp0, 1.0)
    alpha0_rows = per_row(alpha0)
    z1 = z - alpha0_rows * q

    prod1 = product(z1, ah_ref, al_ref)
    exchange_start(3, prod1)
    residual = right_side - alpha0_rows * image
    rz = sums_of(residual, local_z - alpha0_rows * local_q) + ROOT * jnp.sum(
        (own - alpha0 * own_q) * (mean - alpha0 * mean_q), axis=0, keepdims=True
    )
    zz = sums_of(z1, prod1)
    zd = sums_of(z1, prod)
    gx_begin(1, jnp.where(sub == 0, rz, jnp.where(sub == 1, zz, zd)))
    z_begin(1, gx_total(1))
    image1 = exchange_end(3)
    last = z_total(1)
    rz1 = last[0:1]
    beta = rz1 / jnp.where(valid, rz0, 1.0)
    energy = last[1:2] + 2.0 * beta * last[2:3] + beta * beta * dp0
    alpha1 = rz1 / jnp.where(valid, energy, 1.0)
    alpha1_rows = per_row(alpha1)
    beta_rows = per_row(beta)
    sol_ref[...] = alpha0_rows * z + alpha1_rows * (z1 + beta_rows * z)
    res_ref[...] = residual - alpha1_rows * (image1 + beta_rows * image)
    for copy in started:
        copy.wait_send()


def iterate(n_grp, n_sub, *args):
    n_z = n_sub // X_DIM
    n_gx = n_grp * X_DIM
    out = jax.ShapeDtypeStruct((R, M), F32)
    dma = pltpu.SemaphoreType.DMA
    return pl.pallas_call(
        iterate_kernel,
        out_shape=(out, out),
        in_specs=[vmem()] * len(args),
        out_specs=(vmem(), vmem()),
        scratch_shapes=[
            pltpu.VMEM((M, M), BF16),
            pltpu.VMEM((M, M), BF16),
            pltpu.VMEM((M, M), F32),
            pltpu.VMEM((M, 4 * BW), BF16),
            pltpu.VMEM((4 * BW, M), BF16),
            pltpu.VMEM((BW, M), F32),
            pltpu.VMEM((BW, BW), F32),
            pltpu.VMEM((BW, BW), F32),
            pltpu.VMEM((5, 2, R, M // 2), F32),
            pltpu.VMEM((5, 2, R, M // 2), F32),
            pltpu.VMEM((n_grp, 8, BW), F32),
            pltpu.VMEM((2, 3, n_grp, 8, BW), F32),
            pltpu.VMEM((8, BW), F32),
            pltpu.VMEM((2, 8, BW), F32),
            pltpu.VMEM((2, n_gx, 8, BW), F32),
            pltpu.VMEM((2, n_z, 8, BW), F32),
            dma((5, 2)),
            dma((5, 2)),
            dma((n_grp,)),
            dma((n_grp,)),
            dma((2, 3, n_grp)),
            dma((2, 3, n_grp)),
            dma((2,)),
            dma((2,)),
            dma((2, n_gx)),
            dma((2, n_gx)),
            dma((2, n_z)),
            dma((2, n_z)),
        ],
        compiler_params=pltpu.CompilerParams(
            collective_id=0, has_side_effects=True, vmem_limit_bytes=40 * MIB
        ),
        cost_estimate=pl.CostEstimate(
            flops=2_000_000_000, bytes_accessed=10 * MIB, transcendentals=0
        ),
        name="iterate",
    )(*args)


def body(schur, loads, block_map, primal_map, disk_mask):
    a_high, a_low, x, inv, pivot, face, tile = invert(
        block_map[0], primal_map[0], schur[0, 0], loads[0, 0], disk_mask[0]
    )
    sol, res = iterate(
        lax.axis_size("grp"), lax.axis_size("sub"), face, tile, a_high, a_low, x, inv, pivot
    )
    return sol[None, None], res[None, None]


def solution(mesh):
    in_specs = (
        P("sub", "grp", None, None),
        P("sub", "grp", None, None),
        P("sub", "grp", None),
        P("sub", "grp", None),
        P("sub", "grp", None),
    )
    out_specs = (P("sub", "grp", None, None), P("sub", "grp", None, None))
    return jax.shard_map(body, mesh=mesh, in_specs=in_specs, out_specs=out_specs, check_vma=False)
```

time: 132 us -> 117 us (0.89)
  Pallas kernels: 125 us -> 110 us
    pallas_call x2 -> x1, Pallas kernels: 51.3 us -> 36.4 us  [invert(): pl.pallas_call(invert_kernel, out_shape=(arr((M, M), BF16), arr((M, M), B...]
    unnamed x16 -> x12, local copies, waits for them, and re-layouts: 6.55 us -> 6.53 us
where the time goes in v3:
time: 117 us
  Pallas kernels  110 us (94%)
  local copies, waits for them, and re-layouts  6.53 us (6%)
    pallas_call x1, Pallas kernels, iterate(): pl.pallas_call(iterate_kernel, out_shape=(out, out), in_specs=[vmem()] *...  73.6 us
    pallas_call x1, Pallas kernels, invert(): pl.pallas_call(invert_kernel, out_shape=(arr((M, M), BF16), arr((M, M), B...  36.4 us
    unnamed x12, local copies, waits for them, and re-layouts  6.53 us

profile of v3, /device:TPU:1, one launch (start us, length us, event | category | flops | bytes accessed | tf_op | source)
XLA Modules:
  0.0 117.1 jit_solution(7706672488486089323)
XLA Ops:
  0.6 0.0 copy-start
  0.6 2.2 %copy-done = f32[1,1,1024,1024]{3,2,1,0:T(8,128)S(1)} copy-done((f32[1,1,1024,1024]{3,2,1,0:T(8,128)S(1)}, f32[1,1,1024,1024]{3,2,1,0:T(8,128)}, u32[]{:S(2)}) %copy-start) | copy-done | bytes 4194328
  2.8 0.0 copy-start.1
  2.8 0.9 copy-done.1
  3.8 0.0 copy-start.2
  3.8 0.7 copy-done.2
  4.5 0.0 copy-start.3
  4.5 0.7 copy-done.3
  5.1 0.0 copy-start.4
  5.1 0.7 copy-done.4
  5.8 36.4 %invert.1 = (bf16[1024,1024]{1,0:T(8,128)(2,1)S(1)}, bf16[1024,1024]{1,0:T(8,128)(2,1)S(1)}, f32[1152,1152]{1,0:T(8,128)S(1)}, f32[128,128]{1,0:T(8,128)S(1)}, f...) custom-call(s32[1,8]{1,0:T(1,128)S(1)} %bitcast.12, s32[1,8]{1,0:T(1,128)S(1)} %bitcast.13, ...), custom_call_target="tpu_custom_call" | custom-call | flops 20000000000 | bytes 12582912 | tf_op jit(solution)/shard_map/invert/pallas_call | solution.py:261
  42.2 73.6 %iterate.1 = (f32[64,1024]{1,0:T(8,128)S(1)}, f32[64,1024]{1,0:T(8,128)S(1)}) custom-call(f32[64,1024]{1,0:T(8,128)S(1)} %get-tuple-element.11.loads_ref, f32[8,128]{1,0:T(8,128)S(1)} %get-tuple-element.12.tile_ref, bf16[1024,1024]{1,0:T(8,128)(2,1)S(1)} %get-tuple-element.13.ah_ref, bf16[1024,1024]{1,0:T(8,128)(2,1)S(1)} %get-tuple-element.14.al_ref, ...), custom_call_target="tpu_custom_call" | custom-call | flops 2000000000 | bytes 10485760 | tf_op jit(solution)/shard_map/iterate/pallas_call | solution.py:573
  115.7 0.7 copy.9
  116.4 0.7 copy.10
Async XLA Ops:
  0.6 2.2 %copy-start = (f32[1,1,1024,1024]{3,2,1,0:T(8,128)S(1)}, f32[1,1,1024,1024]{3,2,1,0:T(8,128)}, u32[]{:S(2)}) copy-start(f32[1,1,1024,1024]{3,2,1,0:T(8,128)} %param.5) | copy-start | bytes 12582916
  2.8 0.9 copy-start.1
  3.8 0.7 copy-start.2
  4.5 0.7 copy-start.3
  5.1 0.7 copy-start.4

commit v4 on v3

--- a/solution.py
+++ b/solution.py
@@ -17,6 +17,7 @@
 X_DIM = 4
 FIRST = NB - 2
 ROOT = BW ** 0.5
+LOWEST = -3e38
 MIB = 1 << 20
 
 
@@ -46,59 +47,35 @@
     return jnp.broadcast_to(v, (8, BW))
 
 
-def recip(a):
-    r = pltpu.reciprocal(a, approx=True)
-    return r * (2.0 - a * r)
-
-
-def small_mm(a, b):
-    out = []
-    for i in range(len(a)):
-        row = []
-        for j in range(len(b[0])):
-            t = a[i][0] * b[0][j]
-            for l in range(1, len(b)):
-                t = t + a[i][l] * b[l][j]
-            row.append(t)
-        out.append(row)
-    return out
-
-
-def small_inverse(d):
-    n = len(d)
-    if n == 2:
-        a, b, e = d[0][0], d[0][1], d[1][1]
-        r = recip(a * e - b * b)
-        o = -(b * r)
-        return [[e * r, o], [o, a * r]]
-    h = n // 2
-    a = small_inverse([row[:h] for row in d[:h]])
-    b = [row[h:] for row in d[:h]]
-    t = small_mm(a, b)
-    s = [[None] * h for _ in range(h)]
-    for i in range(h):
-        for j in range(i, h):
-            u = b[0][i] * t[0][j]
-            for l in range(1, h):
-                u = u + b[l][i] * t[l][j]
-            s[i][j] = d[h + i][h + j] - u
-            s[j][i] = s[i][j]
-    s = small_inverse(s)
-    ts = small_mm(t, s)
-    r = [[None] * n for _ in range(n)]
-    for i in range(h):
-        for j in range(h):
-            r[h + i][h + j] = s[i][j]
-            r[i][h + j] = -ts[i][j]
-            r[h + j][i] = r[i][h + j]
-    for i in range(h):
-        for j in range(i, h):
-            u = a[i][j]
-            for l in range(h):
-                u = u + ts[i][l] * t[j][l]
-            r[i][j] = u
-            r[j][i] = u
-    return r
+def column_inverse(c, sub):
+    for j in range(0, 8, 2):
+        at_a, at_b = sub == j, sub == j + 1
+        fa, fb = c[j], c[j + 1]
+        a = spread(fa[j : j + 1, :])
+        b = spread(fb[j : j + 1, :])
+        e = spread(fb[j + 1 : j + 2, :])
+        det = a * e - b * b
+        r1 = pltpu.reciprocal(det, approx=True)
+        t = 2.0 - det * r1
+        r = r1 * t
+        new = []
+        for l in range(8):
+            if l == j:
+                v = fa * e - fb * b
+                new.append(jnp.where(at_a, e * r, jnp.where(at_b, -(b * r), -(v * r))))
+            elif l == j + 1:
+                v = fb * a - fa * b
+                new.append(jnp.where(at_a, -(b * r), jnp.where(at_b, a * r, -(v * r))))
+            else:
+                ra = spread(c[l][j : j + 1, :])
+                rb = spread(c[l][j + 1 : j + 2, :])
+                ua = e * ra - b * rb
+                ub = a * rb - b * ra
+                v = fa * ua + fb * ub
+                rest = c[l] - (v * r1) * t
+                new.append(jnp.where(at_a, ua * r, jnp.where(at_b, ub * r, rest)))
+        c = new
+    return c
 
 
 def dense_inverse(x, n, beside=()):
@@ -109,34 +86,26 @@
     sub = lax.broadcasted_iota(jnp.int32, (8, BW), 0)
     for q in range(groups):
         k = 8 * q
-        rows = [spread(xs[q][j : j + 1, :]) for j in range(8)]
-        d = [[None] * 8 for _ in range(8)]
-        for i in range(8):
-            for j in range(i, 8):
-                d[i][j] = spread(rows[i][:, k + j : k + j + 1])
-                d[j][i] = d[i][j]
-        cols = [[spread(xs[i][:, k + j : k + j + 1]) for j in range(8)] for i in range(groups)]
-        r = small_inverse(d)
-        p = []
-        for i in range(8):
-            u = r[i][0] * rows[0]
-            for j in range(1, 8):
-                u = u + r[i][j] * rows[j]
+        others = [(q + 1 + i) % groups for i in range(groups - 1)]
+        own = [jnp.maximum(spread(xs[q][:, k + j : k + j + 1]), LOWEST) for j in range(8)]
+        cols = {i: [spread(xs[i][:, k + j : k + j + 1]) for j in range(8)] for i in others}
+        pivots = (lane >= k) & (lane < k + 8)
+        r = column_inverse(own, sub)
+        rows = [
+            jnp.where(pivots, (lane == k + j).astype(F32), spread(xs[q][j : j + 1, :]))
+            for j in range(8)
+        ]
+        p = r[0] * rows[0]
+        for j in range(1, 8):
+            p = p + r[j] * rows[j]
+        lines = [spread(p[j : j + 1, :]) for j in range(8)]
+        new = [None] * groups
+        new[q] = p
+        for i in others:
+            y = jnp.where(pivots, 0.0, xs[i])
             for j in range(8):
-                u = jnp.where(lane == k + j, r[i][j], u)
-            p.append(u)
-        pivots = (lane >= k) & (lane < k + 8)
-        new = []
-        for i in range(groups):
-            if i == q:
-                y = p[0]
-                for j in range(1, 8):
-                    y = jnp.where(sub == j, p[j], y)
-            else:
-                y = jnp.where(pivots, 0.0, xs[i])
-                for j in range(8):
-                    y = y - cols[i][j] * p[j]
-            new.append(y)
+                y = y - cols[i][j] * lines[j]
+            new[i] = y
         xs = new
         if beside:
             beside.pop(0)()
@@ -168,22 +137,22 @@
 
 def elimination(x, col, rhs, panel, inv, here):
     def rows():
-        panel[...] = dot(four(inv[...], 1), four(x[here, :M], 0))
-        col[...] = four(x[:M, here], 1)
+        panel[...] = dot(four(inv[...], 1), four(x[here, :], 0))
+        col[...] = four(x[:, here], 1)
         x[:, here] = jnp.zeros((x.shape[0], BW), F32)
-        rhs[:, :M] = four(panel[...], 0)
+        rhs[...] = four(panel[...], 0)
         rhs[:, here] = four(inv[...], 0)
 
     def block(n):
         cols = slice(n * 256, (n + 1) * 256)
 
         def work():
-            x[:M, cols] = x[:M, cols] - dot(col[...], rhs[:, cols])
+            x[:, cols] = x[:, cols] - dot(col[...], rhs[:, cols])
 
         return work
 
     def finish():
-        x[here, :M] = panel[...]
+        x[here, :] = panel[...]
         x[here, here] = inv[...]
 
     return rows, [block(n) for n in range(4)], finish
@@ -191,6 +160,12 @@
 
 def nothing():
     pass
+
+
+def next_pivot(x, inv, pivot, inverse, here, after):
+    inv[...] = inverse
+    p = dot(four(inverse, 1), four(x[here, after], 0))
+    pivot[...] = x[after, after] - dot(four(x[after, here], 1), four(p, 0))
 
 
 def pivot_step(x, col, rhs, panel, inv, pivot, last, here, after):
@@ -201,10 +176,10 @@
         work += [block, nothing, nothing]
     inverse = dense_inverse(pivot[...], BW, work)
     finish()
-    inv[...] = inverse
-    if after is not None:
-        p = dot(four(inverse, 1), four(x[here, after], 0))
-        pivot[...] = x[after, after] - dot(four(x[after, here], 1), four(p, 0))
+    if after is None:
+        inv[...] = inverse
+    else:
+        next_pivot(x, inv, pivot, inverse, here, after)
 
 
 def invert_kernel(
@@ -216,24 +191,33 @@
     eye = lax.broadcasted_iota(jnp.int32, (BW, BW), 0) == lax.broadcasted_iota(
         jnp.int32, (BW, BW), 1
     )
-    for f in range(NB):
+
+    def load(f, h):
         row_at = pl.multiple_of(source[f] * BW, BW)
-        face_ref[:, f * BW : (f + 1) * BW] = loads_ref[:, pl.ds(row_at, BW)]
-        for h in range(NB):
-            col_at = pl.multiple_of(source[h] * BW, BW)
-            block = schur_ref[pl.ds(row_at, BW), pl.ds(col_at, BW)]
-            if f == h:
-                penalty = 0.1 * mask_ref[:, pl.ds(col_at, BW)].astype(F32)
-                block = block + jnp.where(eye, penalty, 0.0)
-            x[f * BW : (f + 1) * BW, h * BW : (h + 1) * BW] = block
-            sums[f : f + 1, h * BW : (h + 1) * BW] = jnp.sum(block, axis=0, keepdims=True)
-            high, low = split(block)
-            ah_ref[f * BW : (f + 1) * BW, h * BW : (h + 1) * BW] = high
-            al_ref[f * BW : (f + 1) * BW, h * BW : (h + 1) * BW] = low
-    x[M:, :] = jnp.zeros((BW, M + BW), F32)
-    x[:M, M:] = jnp.zeros((M, BW), F32)
-    inv[...] = jnp.zeros((BW, BW), F32)
-    pivot[...] = x[0:BW, 0:BW]
+        col_at = pl.multiple_of(source[h] * BW, BW)
+        block = schur_ref[pl.ds(row_at, BW), pl.ds(col_at, BW)]
+        if f == h:
+            penalty = 0.1 * mask_ref[:, pl.ds(col_at, BW)].astype(F32)
+            block = block + jnp.where(eye, penalty, 0.0)
+        return block
+
+    def place(f):
+        def work():
+            rows = slice(f * BW, (f + 1) * BW)
+            at_f = pl.multiple_of(source[f] * BW, BW)
+            face_ref[:, rows] = loads_ref[:, pl.ds(at_f, BW)]
+            for h in range(NB):
+                cols = slice(h * BW, (h + 1) * BW)
+                block = load(f, h)
+                x[rows, cols] = block
+                sums[f : f + 1, cols] = jnp.sum(block, axis=0, keepdims=True)
+                ah_ref[rows, cols], al_ref[rows, cols] = split(block)
+
+        return work
+
+    first = slice(0, BW)
+    inverse = dense_inverse(load(0, 0), BW, [place(f) for f in range(NB)])
+    next_pivot(x, inv, pivot, inverse, first, slice(BW, 2 * BW))
 
     sub = lax.broadcasted_iota(jnp.int32, (8, BW), 0)
     lane = lax.broadcasted_iota(jnp.int32, (8, BW), 1)
@@ -247,11 +231,10 @@
     tile_ref[...] = dot_hi(block_sums, primal, ((1,), (0,))) + shifted
 
     def step(k, carry):
-        last = at(lax.rem(k + NB, NB + 1))
-        pivot_step(x, col, rhs, panel, inv, pivot, last, at(k), at(k + 1))
+        pivot_step(x, col, rhs, panel, inv, pivot, at(k - 1), at(k), at(k + 1))
         return carry
 
-    lax.fori_loop(0, FIRST, step, 0)
+    lax.fori_loop(1, FIRST, step, 0)
 
 
 def invert(block_map, primal_map, schur, loads, mask):
@@ -261,14 +244,14 @@
     return pl.pallas_call(
         invert_kernel,
         out_shape=(
-            arr((M, M), BF16), arr((M, M), BF16), arr((M + BW, M + BW)), arr((BW, BW)),
+            arr((M, M), BF16), arr((M, M), BF16), arr((M, M)), arr((BW, BW)),
             arr((BW, BW)), arr((R, M)), arr((8, BW)),
         ),
         in_specs=[smem(), smem(), vmem(), vmem(), vmem()],
         out_specs=(vmem(),) * 7,
         scratch_shapes=[
             pltpu.VMEM((M, 4 * BW), BF16),
-            pltpu.VMEM((4 * BW, M + BW), BF16),
+            pltpu.VMEM((4 * BW, M), BF16),
             pltpu.VMEM((BW, M), F32),
             pltpu.VMEM((8, M), F32),
         ],
@@ -440,7 +423,7 @@
     def piece(k):
         return slice(k * BW, (k + 1) * BW)
 
-    x[...] = x_ref[:M, :M]
+    x[...] = x_ref[...]
     inv[...] = inv_ref[...]
     pivot[...] = pivot_ref[...]
     pivot_step(

time: 117 us -> 110 us (0.940)
  Pallas kernels: 110 us -> 103 us
    pallas_call x1, Pallas kernels: 36.4 us -> 29.8 us  [invert(): pl.pallas_call(invert_kernel, out_shape=(arr((M, M), BF16), arr((M, M), B...]
where the time goes in v4:
time: 110 us
  Pallas kernels  103 us (94%)
  local copies, waits for them, and re-layouts  6.53 us (6%)
    pallas_call x1, Pallas kernels, iterate(): pl.pallas_call(iterate_kernel, out_shape=(out, out), in_specs=[vmem()] *...  72.9 us
    pallas_call x1, Pallas kernels, invert(): pl.pallas_call(invert_kernel, out_shape=(arr((M, M), BF16), arr((M, M), B...  29.8 us
    unnamed x12, local copies, waits for them, and re-layouts  6.53 us

profile of v4, /device:TPU:1, one launch (start us, length us, event | category | flops | bytes accessed | tf_op | source)
XLA Modules:
  0.0 109.8 jit_solution(1732904192537045721)
XLA Ops:
  0.6 0.0 copy-start
  0.6 2.2 %copy-done = f32[1,1,1024,1024]{3,2,1,0:T(8,128)S(1)} copy-done((f32[1,1,1024,1024]{3,2,1,0:T(8,128)S(1)}, f32[1,1,1024,1024]{3,2,1,0:T(8,128)}, u32[]{:S(2)}) %copy-start) | copy-done | bytes 4194328
  2.8 0.0 copy-start.1
  2.8 0.9 copy-done.1
  3.8 0.0 copy-start.2
  3.8 0.7 copy-done.2
  4.5 0.0 copy-start.3
  4.5 0.7 copy-done.3
  5.1 0.0 copy-start.4
  5.1 0.7 copy-done.4
  5.8 29.8 %invert.1 = (bf16[1024,1024]{1,0:T(8,128)(2,1)S(1)}, bf16[1024,1024]{1,0:T(8,128)(2,1)S(1)}, f32[1024,1024]{1,0:T(8,128)S(1)}, f32[128,128]{1,0:T(8,128)S(1)}, f...) custom-call(s32[1,8]{1,0:T(1,128)S(1)} %bitcast.12, s32[1,8]{1,0:T(1,128)S(1)} %bitcast.13, ...), custom_call_target="tpu_custom_call" | custom-call | flops 20000000000 | bytes 12582912 | tf_op jit(solution)/shard_map/invert/pallas_call | solution.py:244
  35.6 72.9 %iterate.1 = (f32[64,1024]{1,0:T(8,128)S(1)}, f32[64,1024]{1,0:T(8,128)S(1)}) custom-call(f32[64,1024]{1,0:T(8,128)S(1)} %get-tuple-element.11.loads_ref, f32[8,128]{1,0:T(8,128)S(1)} %get-tuple-element.12.tile_ref, bf16[1024,1024]{1,0:T(8,128)(2,1)S(1)} %get-tuple-element.13.ah_ref, bf16[1024,1024]{1,0:T(8,128)(2,1)S(1)} %get-tuple-element.14.al_ref, ...), custom_call_target="tpu_custom_call" | custom-call | flops 2000000000 | bytes 10485760 | tf_op jit(solution)/shard_map/iterate/pallas_call | solution.py:556
  108.4 0.7 copy.9
  109.1 0.7 copy.10
Async XLA Ops:
  0.6 2.2 %copy-start = (f32[1,1,1024,1024]{3,2,1,0:T(8,128)S(1)}, f32[1,1,1024,1024]{3,2,1,0:T(8,128)}, u32[]{:S(2)}) copy-start(f32[1,1,1024,1024]{3,2,1,0:T(8,128)} %param.5) | copy-start | bytes 12582916
  2.8 0.9 copy-start.1
  3.8 0.7 copy-start.2
  4.5 0.7 copy-start.3
  5.1 0.7 copy-start.4

commit v5 on v4

--- a/solution.py
+++ b/solution.py
@@ -15,7 +15,7 @@
 NB = 8
 C = 32
 X_DIM = 4
-FIRST = NB - 2
+FIRST = NB - 4
 ROOT = BW ** 0.5
 LOWEST = -3e38
 MIB = 1 << 20
@@ -420,6 +420,12 @@
         wide = dot_hi(tile, jnp.ones((8, BW), F32), ((0,), (0,)))[:R]
         return jnp.concatenate([wide] * NB, 1)
 
+    def weight_args(side):
+        return (
+            weights_out, weights_in.at[1 - side], w_send.at[side], w_recv.at[1 - side],
+            ((left, right)[side], g),
+        )
+
     def piece(k):
         return slice(k * BW, (k + 1) * BW)
 
@@ -427,18 +433,23 @@
     inv[...] = inv_ref[...]
     pivot[...] = pivot_ref[...]
     pivot_step(
-        x, col, rhs, panel, inv, pivot, piece(NB - 3), piece(NB - 2), piece(NB - 1)
+        x, col, rhs, panel, inv, pivot, piece(FIRST - 1), piece(FIRST), piece(FIRST + 1)
     )
     pl.semaphore_wait(barrier, len(partners))
     tiles[g] = tile_ref[...]
     for d in range(1, n_grp):
         start(tiles.at[g], tiles.at[g], tile_send.at[d], tile_recv.at[g], (s, around(d)))
     exchange_start(4, loads_ref[...])
-    pivot_step(x, col, rhs, panel, inv, pivot, piece(NB - 2), piece(NB - 1), None)
-    rows, _, finish = elimination(x, col, rhs, panel, inv, piece(NB - 1))
-    rows()
-    finish()
-    col[M - BW :, :] = jnp.zeros((BW, 4 * BW), BF16)
+
+    def step(k, carry):
+        pivot_step(x, col, rhs, panel, inv, pivot, at(k - 1), at(k), at(k + 1))
+        return carry
+
+    lax.fori_loop(FIRST + 1, NB - 1, step, 0)
+    right_side = exchange_end(4)
+    weighted = 0.5 * right_side
+    mean = averages(weighted)
+    avg_begin(0, mean)
 
     for d in range(1, n_grp):
         o = around(d)
@@ -455,19 +466,17 @@
     )[:, :C]
     primal = tile_ref[:, C : 2 * C]
     weights = dot_hi(dot_hi(primal, coarse_inverse, ((1,), (0,))), primal_all, ((1,), (1,)))
+    pivot_step(x, col, rhs, panel, inv, pivot, piece(NB - 2), piece(NB - 1), None)
+    weights_out[...] = jnp.concatenate([weights, jnp.zeros((8, BW - n_grp * 8), F32)], 1)
+    for side in range(2):
+        start(*weight_args(side))
+    rows, _, finish = elimination(x, col, rhs, panel, inv, piece(NB - 1))
+    rows()
+    finish()
+    col[M - BW :, :] = jnp.zeros((BW, 4 * BW), BF16)
     for n in range(4):
         cols = slice(n * 256, (n + 1) * 256)
         xh_ref[:, cols], xl_ref[:, cols] = split(x[:, cols] - dot(col[...], rhs[:, cols]))
-
-    def weight_args(side):
-        return (
-            weights_out, weights_in.at[1 - side], w_send.at[side], w_recv.at[1 - side],
-            ((left, right)[side], g),
-        )
-
-    weights_out[...] = jnp.concatenate([weights, jnp.zeros((8, BW - n_grp * 8), F32)], 1)
-    for side in range(2):
-        start(*weight_args(side))
 
     def amounts(e):
         avg_end(e)
@@ -479,11 +488,6 @@
 
     def expand(tile):
         return dot_hi(tile[:, :R], blocks, ((0,), (0,)))
-
-    right_side = exchange_end(4)
-    weighted = 0.5 * right_side
-    mean = averages(weighted)
-    avg_begin(0, mean)
 
     local_z = 0.5 * product(weighted, xh_ref, xl_ref)
     exchange_start(0, local_z)

time: 110 us -> 107 us (0.973)
  Pallas kernels: 103 us -> 99.7 us
    pallas_call x1, Pallas kernels: 29.8 us -> 20.4 us  [invert(): pl.pallas_call(invert_kernel, out_shape=(arr((M, M), BF16), arr((M, M), B...]
    pallas_call x1, Pallas kernels: 72.9 us -> 79.3 us  [iterate(): pl.pallas_call(iterate_kernel, out_shape=(out, out), in_specs=[vmem()] *...]
where the time goes in v5:
time: 107 us
  Pallas kernels  99.7 us (93%)
  local copies, waits for them, and re-layouts  6.53 us (6%)
    pallas_call x1, Pallas kernels, iterate(): pl.pallas_call(iterate_kernel, out_shape=(out, out), in_specs=[vmem()] *...  79.3 us
    pallas_call x1, Pallas kernels, invert(): pl.pallas_call(invert_kernel, out_shape=(arr((M, M), BF16), arr((M, M), B...  20.4 us
    unnamed x12, local copies, waits for them, and re-layouts  6.53 us

profile of v5, /device:TPU:1, one launch (start us, length us, event | category | flops | bytes accessed | tf_op | source)
XLA Modules:
  0.0 106.9 jit_solution(8335565638279142966)
XLA Ops:
  0.6 0.0 copy-start
  0.6 2.2 %copy-done = f32[1,1,1024,1024]{3,2,1,0:T(8,128)S(1)} copy-done((f32[1,1,1024,1024]{3,2,1,0:T(8,128)S(1)}, f32[1,1,1024,1024]{3,2,1,0:T(8,128)}, u32[]{:S(2)}) %copy-start) | copy-done | bytes 4194328
  2.8 0.0 copy-start.1
  2.8 0.9 copy-done.1
  3.8 0.0 copy-start.2
  3.8 0.7 copy-done.2
  4.5 0.0 copy-start.3
  4.5 0.7 copy-done.3
  5.1 0.0 copy-start.4
  5.1 0.7 copy-done.4
  5.8 20.4 %invert.1 = (bf16[1024,1024]{1,0:T(8,128)(2,1)S(1)}, bf16[1024,1024]{1,0:T(8,128)(2,1)S(1)}, f32[1024,1024]{1,0:T(8,128)S(1)}, f32[128,128]{1,0:T(8,128)S(1)}, f...) custom-call(s32[1,8]{1,0:T(1,128)S(1)} %bitcast.12, s32[1,8]{1,0:T(1,128)S(1)} %bitcast.13, ...), custom_call_target="tpu_custom_call" | custom-call | flops 20000000000 | bytes 12582912 | tf_op jit(solution)/shard_map/invert/pallas_call | solution.py:244
  26.2 79.3 %iterate.1 = (f32[64,1024]{1,0:T(8,128)S(1)}, f32[64,1024]{1,0:T(8,128)S(1)}) custom-call(f32[64,1024]{1,0:T(8,128)S(1)} %get-tuple-element.11.loads_ref, f32[8,128]{1,0:T(8,128)S(1)} %get-tuple-element.12.tile_ref, bf16[1024,1024]{1,0:T(8,128)(2,1)S(1)} %get-tuple-element.13.ah_ref, bf16[1024,1024]{1,0:T(8,128)(2,1)S(1)} %get-tuple-element.14.al_ref, ...), custom_call_target="tpu_custom_call" | custom-call | flops 2000000000 | bytes 10485760 | tf_op jit(solution)/shard_map/iterate/pallas_call | solution.py:560
  105.5 0.7 copy.9
  106.2 0.7 copy.10
Async XLA Ops:
  0.6 2.2 %copy-start = (f32[1,1,1024,1024]{3,2,1,0:T(8,128)S(1)}, f32[1,1,1024,1024]{3,2,1,0:T(8,128)}, u32[]{:S(2)}) copy-start(f32[1,1,1024,1024]{3,2,1,0:T(8,128)} %param.5) | copy-start | bytes 12582916
  2.8 0.9 copy-start.1
  3.8 0.7 copy-start.2
  4.5 0.7 copy-start.3
  5.1 0.7 copy-start.4

commit v6 on v5

--- a/solution.py
+++ b/solution.py
@@ -514,9 +514,9 @@
     half = 0.5 * image
     mean_q = averages(half)
     avg_begin(1, mean_q)
+    z_begin(0, gx_total(0))
     local_q = 0.5 * product(half, xh_ref, xl_ref)
     exchange_start(2, local_q)
-    z_begin(0, gx_total(0))
     own_q, both_q = amounts(1)
     coarse_q = 0.5 * expand(both_q)
     q = exchange_end(2) + coarse_q

time: 107 us -> 107 us (level); the launches traced: 107 us -> 105 us
  Pallas kernels: 99.7 us -> 98 us
    pallas_call x1, Pallas kernels: 79.3 us -> 77.6 us  [iterate(): pl.pallas_call(iterate_kernel, out_shape=(out, out), in_specs=[vmem()] *...]
where the time goes in v6:
time: 107 us; the launch traced here: 105 us
  Pallas kernels  98 us (92%)
  local copies, waits for them, and re-layouts  6.53 us (6%)
    pallas_call x1, Pallas kernels, iterate(): pl.pallas_call(iterate_kernel, out_shape=(out, out), in_specs=[vmem()] *...  77.6 us
    pallas_call x1, Pallas kernels, invert(): pl.pallas_call(invert_kernel, out_shape=(arr((M, M), BF16), arr((M, M), B...  20.4 us
    unnamed x12, local copies, waits for them, and re-layouts  6.53 us

profile of v6, /device:TPU:1, one launch (start us, length us, event | category | flops | bytes accessed | tf_op | source)
XLA Modules:
  0.0 105.2 jit_solution(3070656523466305319)
XLA Ops:
  0.6 0.0 copy-start
  0.6 2.2 %copy-done = f32[1,1,1024,1024]{3,2,1,0:T(8,128)S(1)} copy-done((f32[1,1,1024,1024]{3,2,1,0:T(8,128)S(1)}, f32[1,1,1024,1024]{3,2,1,0:T(8,128)}, u32[]{:S(2)}) %copy-start) | copy-done | bytes 4194328
  2.8 0.0 copy-start.1
  2.8 0.9 copy-done.1
  3.8 0.0 copy-start.2
  3.8 0.7 copy-done.2
  4.5 0.0 copy-start.3
  4.5 0.7 copy-done.3
  5.1 0.0 copy-start.4
  5.1 0.7 copy-done.4
  5.8 20.4 %invert.1 = (bf16[1024,1024]{1,0:T(8,128)(2,1)S(1)}, bf16[1024,1024]{1,0:T(8,128)(2,1)S(1)}, f32[1024,1024]{1,0:T(8,128)S(1)}, f32[128,128]{1,0:T(8,128)S(1)}, f...) custom-call(s32[1,8]{1,0:T(1,128)S(1)} %bitcast.12, s32[1,8]{1,0:T(1,128)S(1)} %bitcast.13, ...), custom_call_target="tpu_custom_call" | custom-call | flops 20000000000 | bytes 12582912 | tf_op jit(solution)/shard_map/invert/pallas_call | solution.py:244
  26.2 77.6 %iterate.1 = (f32[64,1024]{1,0:T(8,128)S(1)}, f32[64,1024]{1,0:T(8,128)S(1)}) custom-call(f32[64,1024]{1,0:T(8,128)S(1)} %get-tuple-element.11.loads_ref, f32[8,128]{1,0:T(8,128)S(1)} %get-tuple-element.12.tile_ref, bf16[1024,1024]{1,0:T(8,128)(2,1)S(1)} %get-tuple-element.13.ah_ref, bf16[1024,1024]{1,0:T(8,128)(2,1)S(1)} %get-tuple-element.14.al_ref, ...), custom_call_target="tpu_custom_call" | custom-call | flops 2000000000 | bytes 10485760 | tf_op jit(solution)/shard_map/iterate/pallas_call | solution.py:560
  103.8 0.7 copy.9
  104.5 0.7 copy.10
Async XLA Ops:
  0.6 2.2 %copy-start = (f32[1,1,1024,1024]{3,2,1,0:T(8,128)S(1)}, f32[1,1,1024,1024]{3,2,1,0:T(8,128)}, u32[]{:S(2)}) copy-start(f32[1,1,1024,1024]{3,2,1,0:T(8,128)} %param.5) | copy-start | bytes 12582916
  2.8 0.9 copy-start.1
  3.8 0.7 copy-start.2
  4.5 0.7 copy-start.3
  5.1 0.7 copy-start.4
